TPU v7x, 32 devices: a whole 2x2x4 slice. The times are simulated.
32 devices in a mesh: dp: 8 (over y, x, core), seq: 4 (over z).
Axes of the slice: x: 2, y: 2, z: 4, core: 2. Of those that a mesh axis runs over, the one named last changes fastest.
Arguments:
- tokens: bfloat16 [16, 2048, 576], P('dp', 'seq'), may hold values from -54 to 54
- positions: int32 [16, 2048], P('dp', 'seq'), may hold values from 0 to 2047, as said below
- cotangent: bfloat16 [16, 2048, 576], P('dp', 'seq'), may hold values from -6 to 6
- balance: float32 [576], P('seq'), may hold values from 0.5 to 1.5
- projector: float32 [576, 960], P('seq'), may hold values from -0.25 to 0.25
- combiner: float32 [576, 576], P('seq'), may hold values from -4 to 4
- leveler: float32 [576], P('seq'), may hold values from 0.5 to 1.5
- expander: float32 [576, 3072], P('seq'), may hold values from -0.25 to 0.25
- reducer: float32 [1536, 576], P('seq'), may hold values from -0.15625 to 0.15625
- mean_balance: float32 [576], P('seq'), may hold values from -724.07733 to 724.07733
- mean_projector: float32 [576, 960], P('seq'), may hold values from -325.8348 to 325.8348
- mean_combiner: float32 [576, 576], P('seq'), may hold values from -11.2 to 11.2
- mean_leveler: float32 [576], P('seq'), may hold values from -162.9174 to 162.9174
- mean_expander: float32 [576, 3072], P('seq'), may hold values from -119.47276 to 119.47276
- mean_reducer: float32 [1536, 576], P('seq'), may hold values from -119.47276 to 119.47276
- square_balance: float32 [576], P('seq'), may hold values from 6553.6 to 104857.6
- square_projector: float32 [576, 960], P('seq'), may hold values from 1310.72 to 20971.52
- square_combiner: float32 [576, 576], P('seq'), may hold values from 1.6 to 25.6
- square_leveler: float32 [576], P('seq'), may hold values from 327.68 to 5242.88
- square_expander: float32 [576, 3072], P('seq'), may hold values from 163.84 to 2621.44
- square_reducer: float32 [1536, 576], P('seq'), may hold values from 163.84 to 2621.44
Outputs:
- layer_out: bfloat16 [16, 2048, 576], P('dp', 'seq')
- tokens_grad: bfloat16 [16, 2048, 576], P('dp', 'seq')
- grad_balance: float32 [576], P('seq')
- grad_projector: float32 [576, 960], P('seq')
- grad_combiner: float32 [576, 576], P('seq')
- grad_leveler: float32 [576], P('seq')
- grad_expander: float32 [576, 3072], P('seq')
- grad_reducer: float32 [1536, 576], P('seq')
- next_balance: float32 [576], P('seq')
- next_projector: float32 [576, 960], P('seq')
- next_combiner: float32 [576, 576], P('seq')
- next_leveler: float32 [576], P('seq')
- next_expander: float32 [576, 3072], P('seq')
- next_reducer: float32 [1536, 576], P('seq')
- newmean_balance: float32 [576], P('seq')
- newmean_projector: float32 [576, 960], P('seq')
- newmean_combiner: float32 [576, 576], P('seq')
- newmean_leveler: float32 [576], P('seq')
- newmean_expander: float32 [576, 3072], P('seq')
- newmean_reducer: float32 [1536, 576], P('seq')
- newsquare_balance: float32 [576], P('seq')
- newsquare_projector: float32 [576, 960], P('seq')
- newsquare_combiner: float32 [576, 576], P('seq')
- newsquare_leveler: float32 [576], P('seq')
- newsquare_expander: float32 [576, 3072], P('seq')
- newsquare_reducer: float32 [1536, 576], P('seq')
Inputs may be any that keep to these rules, and one draw needn't show every extreme that they name: `positions`: in every sequence the first token has position 0, and each later token has either position 0 (a new document begins) or its predecessor's position plus 1; the first sequence is one whole document.
All inputs are finite; a program needn't handle non-finite values.
Results may differ from a plain program's by a relative error of at most 0.025.
Values may be sent and summed in bfloat16 or wider, within the bound.
A program may use at most 448 MiB of HBM per device.

v0:
```python
import jax
import jax.numpy as jnp
from jax import lax
from jax.sharding import PartitionSpec as P

HEADS = 9
KV_HEADS = 3
HEAD_DIM = 64
STEP = 2


norm_eps = 1e-05
rope_base = 100000.0
beta_one = 0.9
beta_two = 0.95
adam_eps = 1e-08
learn_rate = 0.2
decay_rate = 0.1


def rms_scale(values, scales):
    factor = lax.rsqrt(jnp.mean(values * values, axis=-1, keepdims=True) + norm_eps)
    return values * factor * scales


def angles(token_pos):
    exponent = jnp.arange(HEAD_DIM // 2, dtype=jnp.float32) * (2.0 / HEAD_DIM)
    inverse = jnp.power(rope_base, -exponent)
    return token_pos.astype(jnp.float32)[..., None] * inverse


def rotate(values, phases):
    half_dim = values.shape[-1] // 2
    first = values[..., :half_dim]
    second = values[..., half_dim:]
    cosine = jnp.cos(phases)[..., None, :]
    sine_part = jnp.sin(phases)[..., None, :]
    return jnp.concatenate(
        [first * cosine - second * sine_part, second * cosine + first * sine_part], axis=-1
    )


def adam_step(master, grad_total, mean_old, square_old, decays):
    mean_new = beta_one * mean_old + (1.0 - beta_one) * grad_total
    square_new = beta_two * square_old + (1.0 - beta_two) * grad_total * grad_total
    mean_hat = mean_new / (1.0 - beta_one**STEP)
    square_hat = square_new / (1.0 - beta_two**STEP)
    change = mean_hat / (jnp.sqrt(square_hat) + adam_eps)
    if decays:
        change = change + decay_rate * master
    return (master - learn_rate * change, mean_new, square_new)


def on_device(
    tokens,
    positions,
    cotangent,
    balance,
    projector,
    combiner,
    leveler,
    expander,
    reducer,
    mean_balance,
    mean_projector,
    mean_combiner,
    mean_leveler,
    mean_expander,
    mean_reducer,
    square_balance,
    square_projector,
    square_combiner,
    square_leveler,
    square_expander,
    square_reducer,
):
    copies = (
        lax.all_gather(balance.astype(jnp.bfloat16), "seq", axis=0, tiled=True),
        lax.all_gather(projector.astype(jnp.bfloat16), "seq", axis=0, tiled=True),
        lax.all_gather(combiner.astype(jnp.bfloat16), "seq", axis=0, tiled=True),
        lax.all_gather(leveler.astype(jnp.bfloat16), "seq", axis=0, tiled=True),
        lax.all_gather(expander.astype(jnp.bfloat16), "seq", axis=0, tiled=True),
        lax.all_gather(reducer.astype(jnp.bfloat16), "seq", axis=0, tiled=True),
    )
    gain_one = copies[0].astype(jnp.float32)
    proj_copy = copies[1]
    comb_copy = copies[2]
    gain_two = copies[3].astype(jnp.float32)
    expand_copy = copies[4]
    shrink_copy = copies[5]
    seq_count, local_len, model_width = tokens.shape
    row_count = seq_count * local_len
    inner_width = HEADS * HEAD_DIM
    kv_width = KV_HEADS * HEAD_DIM
    group_size = HEADS // KV_HEADS
    full_len = local_len * lax.axis_size("seq")
    inputs = tokens.reshape(row_count, model_width).astype(jnp.float32)
    normed_one, norm_one_back = jax.vjp(rms_scale, inputs, gain_one)
    act_one = normed_one.astype(jnp.bfloat16)
    projected = jnp.dot(act_one, proj_copy, preferred_element_type=jnp.float32)
    phases = angles(positions.reshape(row_count))

    def rotate_tok(values):
        return rotate(values, phases)

    query_rot, query_back = jax.vjp(
        rotate_tok, projected[:, :inner_width].reshape(row_count, HEADS, HEAD_DIM)
    )
    key_rot, key_back = jax.vjp(
        rotate_tok,
        projected[:, inner_width : inner_width + kv_width].reshape(row_count, KV_HEADS, HEAD_DIM),
    )
    queries = query_rot.astype(jnp.bfloat16).reshape(
        seq_count, local_len, KV_HEADS, group_size, HEAD_DIM
    )
    keys_own = key_rot.astype(jnp.bfloat16).reshape(seq_count, local_len, kv_width)
    values_own = (
        projected[:, inner_width + kv_width :]
        .astype(jnp.bfloat16)
        .reshape(seq_count, local_len, kv_width)
    )
    all_keys, all_values = (
        lax.all_gather(keys_own, "seq", axis=1, tiled=True),
        lax.all_gather(values_own, "seq", axis=1, tiled=True),
    )
    query_index = lax.axis_index("seq") * local_len + jnp.arange(local_len, dtype=jnp.int32)
    key_index = jnp.arange(full_len, dtype=jnp.int32)
    lowest = query_index[None, :] - positions

    def visible_of(number):
        return (key_index[None, :] <= query_index[:, None]) & (
            key_index[None, :] >= lowest[number][:, None]
        )

    def scores_of(number, key_block):
        key_heads = key_block[number].reshape(full_len, KV_HEADS, HEAD_DIM)
        raw = jnp.einsum(
            "qgjd,kgd->gjqk", queries[number], key_heads, preferred_element_type=jnp.float32
        )
        return jnp.where(visible_of(number)[None, None], 0.125 * raw, -1e30)

    mixed_list = []
    lse_list = []
    for number in range(seq_count):
        masked = scores_of(number, all_keys)
        top_score = jnp.max(masked, axis=-1, keepdims=True)
        log_total = top_score + jnp.log(
            jnp.sum(jnp.exp(masked - top_score), axis=-1, keepdims=True)
        )
        probs = jnp.where(visible_of(number)[None, None], jnp.exp(masked - log_total), 0.0)
        value_heads = all_values[number].reshape(full_len, KV_HEADS, HEAD_DIM)
        mixed = jnp.einsum(
            "gjqk,kgd->qgjd",
            probs.astype(jnp.bfloat16),
            value_heads,
            preferred_element_type=jnp.float32,
        )
        mixed_list.append(mixed.reshape(local_len, inner_width))
        lse_list.append(log_total)
    heads_out = jnp.concatenate(mixed_list, axis=0).astype(jnp.bfloat16)
    middle = inputs + jnp.dot(heads_out, comb_copy, preferred_element_type=jnp.float32)
    normed_two, norm_two_back = jax.vjp(rms_scale, middle, gain_two)
    act_two = normed_two.astype(jnp.bfloat16)
    gate_up = jnp.dot(act_two, expand_copy, preferred_element_type=jnp.float32)
    ff_width = shrink_copy.shape[0]

    def swiglu(both):
        return jax.nn.silu(both[:, :ff_width]) * both[:, ff_width:]

    active, swiglu_back = jax.vjp(swiglu, gate_up)
    active_low = active.astype(jnp.bfloat16)
    layer_out = (
        middle + jnp.dot(active_low, shrink_copy, preferred_element_type=jnp.float32)
    ).astype(jnp.bfloat16)
    out_grad = cotangent.reshape(row_count, model_width).astype(jnp.float32)
    out_low = out_grad.astype(jnp.bfloat16)
    grad_shrink = jnp.einsum("tf,td->fd", active_low, out_low, preferred_element_type=jnp.float32)
    active_grad = jnp.einsum("td,fd->tf", out_low, shrink_copy, preferred_element_type=jnp.float32)
    (gate_grad,) = swiglu_back(active_grad)
    gate_low = gate_grad.astype(jnp.bfloat16)
    grad_expand = jnp.einsum("td,tf->df", act_two, gate_low, preferred_element_type=jnp.float32)
    act_two_grad = jnp.einsum(
        "tf,df->td", gate_low, expand_copy, preferred_element_type=jnp.float32
    )
    middle_part, grad_gain_two = norm_two_back(act_two_grad)
    mid_grad = out_grad + middle_part
    mid_low = mid_grad.astype(jnp.bfloat16)
    grad_comb = jnp.einsum("ti,td->id", heads_out, mid_low, preferred_element_type=jnp.float32)
    heads_grad = jnp.einsum(
        "td,id->ti", mid_low, comb_copy, preferred_element_type=jnp.float32
    ).astype(jnp.bfloat16)
    heads_grad = heads_grad.reshape(seq_count, local_len, KV_HEADS, group_size, HEAD_DIM)
    back_keys, back_values = (
        lax.all_gather(keys_own, "seq", axis=1, tiled=True),
        lax.all_gather(values_own, "seq", axis=1, tiled=True),
    )
    query_grads = []
    key_grads = []
    value_grads = []
    for number in range(seq_count):
        visible = visible_of(number)[None, None]
        masked = scores_of(number, back_keys)
        probs = jnp.where(visible, jnp.exp(masked - lse_list[number]), 0.0)
        probs_low = probs.astype(jnp.bfloat16)
        key_heads = back_keys[number].reshape(full_len, KV_HEADS, HEAD_DIM)
        value_heads = back_values[number].reshape(full_len, KV_HEADS, HEAD_DIM)
        prob_grad = jnp.einsum(
            "qgjd,kgd->gjqk", heads_grad[number], value_heads, preferred_element_type=jnp.float32
        )
        value_grads.append(
            jnp.einsum(
                "gjqk,qgjd->kgd", probs_low, heads_grad[number], preferred_element_type=jnp.float32
            ).reshape(full_len, kv_width)
        )
        score_grad = (
            probs * (prob_grad - jnp.sum(probs * prob_grad, axis=-1, keepdims=True))
        ).astype(jnp.bfloat16)
        query_grads.append(
            0.125
            * jnp.einsum(
                "gjqk,kgd->qgjd", score_grad, key_heads, preferred_element_type=jnp.float32
            ).reshape(local_len, inner_width)
        )
        key_grads.append(
            0.125
            * jnp.einsum(
                "gjqk,qgjd->kgd", score_grad, queries[number], preferred_element_type=jnp.float32
            ).reshape(full_len, kv_width)
        )
    key_own_grad, value_own_grad = (
        lax.psum_scatter(
            jnp.stack(key_grads).astype(jnp.bfloat16), "seq", scatter_dimension=1, tiled=True
        ).astype(jnp.float32),
        lax.psum_scatter(
            jnp.stack(value_grads).astype(jnp.bfloat16), "seq", scatter_dimension=1, tiled=True
        ).astype(jnp.float32),
    )
    (query_back_grad,) = query_back(
        jnp.concatenate(query_grads, axis=0).reshape(row_count, HEADS, HEAD_DIM)
    )
    (key_back_grad,) = key_back(key_own_grad.reshape(row_count, KV_HEADS, HEAD_DIM))
    proj_grad_low = jnp.concatenate(
        [
            query_back_grad.reshape(row_count, inner_width),
            key_back_grad.reshape(row_count, kv_width),
            value_own_grad.reshape(row_count, kv_width),
        ],
        axis=1,
    ).astype(jnp.bfloat16)
    grad_proj = jnp.einsum("td,tc->dc", act_one, proj_grad_low, preferred_element_type=jnp.float32)
    act_one_grad = jnp.einsum(
        "tc,dc->td", proj_grad_low, proj_copy, preferred_element_type=jnp.float32
    )
    input_part, grad_gain_one = norm_one_back(act_one_grad)
    tokens_grad = (
        (mid_grad + input_part).astype(jnp.bfloat16).reshape(seq_count, local_len, model_width)
    )
    grads = (grad_gain_one, grad_proj, grad_comb, grad_gain_two, grad_expand, grad_shrink)
    slices = (
        lax.psum_scatter(
            grads[0].astype(jnp.bfloat16), "seq", scatter_dimension=0, tiled=True
        ).astype(jnp.float32),
        lax.psum_scatter(
            grads[1].astype(jnp.bfloat16), "seq", scatter_dimension=0, tiled=True
        ).astype(jnp.float32),
        lax.psum_scatter(
            grads[2].astype(jnp.bfloat16), "seq", scatter_dimension=0, tiled=True
        ).astype(jnp.float32),
        lax.psum_scatter(
            grads[3].astype(jnp.bfloat16), "seq", scatter_dimension=0, tiled=True
        ).astype(jnp.float32),
        lax.psum_scatter(
            grads[4].astype(jnp.bfloat16), "seq", scatter_dimension=0, tiled=True
        ).astype(jnp.float32),
        lax.psum_scatter(
            grads[5].astype(jnp.bfloat16), "seq", scatter_dimension=0, tiled=True
        ).astype(jnp.float32),
    )
    totals = (
        lax.psum(slices[0].astype(jnp.bfloat16), "dp").astype(jnp.float32),
        lax.psum(slices[1].astype(jnp.bfloat16), "dp").astype(jnp.float32),
        lax.psum(slices[2].astype(jnp.bfloat16), "dp").astype(jnp.float32),
        lax.psum(slices[3].astype(jnp.bfloat16), "dp").astype(jnp.float32),
        lax.psum(slices[4].astype(jnp.bfloat16), "dp").astype(jnp.float32),
        lax.psum(slices[5].astype(jnp.bfloat16), "dp").astype(jnp.float32),
    )
    masters = (balance, projector, combiner, leveler, expander, reducer)
    means = (mean_balance, mean_projector, mean_combiner, mean_leveler, mean_expander, mean_reducer)
    squares = (
        square_balance,
        square_projector,
        square_combiner,
        square_leveler,
        square_expander,
        square_reducer,
    )
    decay_flags = (False, True, True, False, True, True)
    results = [
        adam_step(
            masters[number], totals[number], means[number], squares[number], decay_flags[number]
        )
        for number in range(6)
    ]
    return (
        layer_out.reshape(seq_count, local_len, model_width),
        tokens_grad,
        totals[0],
        totals[1],
        totals[2],
        totals[3],
        totals[4],
        totals[5],
        results[0][0],
        results[1][0],
        results[2][0],
        results[3][0],
        results[4][0],
        results[5][0],
        results[0][1],
        results[1][1],
        results[2][1],
        results[3][1],
        results[4][1],
        results[5][1],
        results[0][2],
        results[1][2],
        results[2][2],
        results[3][2],
        results[4][2],
        results[5][2],
    )


def solution(mesh):
    placed = (
        P("dp", "seq", None),
        P("dp", "seq"),
        P("dp", "seq", None),
        P("seq"),
        P("seq", None),
        P("seq", None),
        P("seq"),
        P("seq", None),
        P("seq", None),
        P("seq"),
        P("seq", None),
        P("seq", None),
        P("seq"),
        P("seq", None),
        P("seq", None),
        P("seq"),
        P("seq", None),
        P("seq", None),
        P("seq"),
        P("seq", None),
        P("seq", None),
    )
    return jax.shard_map(
        on_device,
        mesh=mesh,
        in_specs=placed,
        out_specs=(
            P("dp", "seq", None),
            P("dp", "seq", None),
            P("seq"),
            P("seq", None),
            P("seq", None),
            P("seq"),
            P("seq", None),
            P("seq", None),
            P("seq"),
            P("seq", None),
            P("seq", None),
            P("seq"),
            P("seq", None),
            P("seq", None),
            P("seq"),
            P("seq", None),
            P("seq", None),
            P("seq"),
            P("seq", None),
            P("seq", None),
            P("seq"),
            P("seq", None),
            P("seq", None),
            P("seq"),
            P("seq", None),
            P("seq", None),
        ),
        check_vma=False,
    )
```

profile of v0, /device:TPU:0, one launch (start us, length us, event | category | flops | bytes accessed | tf_op | source)
XLA Modules:
  0.0 965.9 jit_solution(7312749107047850904)
XLA Ops:
  13.0 13.5 %all-reduce.13 = (bf16[576]{0:T(1024)(128)(2,1)S(1)}, bf16[576]{0:T(1024)(128)(2,1)S(1)}) all-reduce(bf16[576]{0:T(1024)(128)(2,1)S(1)} %dynamic-update-slice, bf16[576]{0:T(1024)(128)(2,1)S(1)} %dynamic-update-slice.1), channel_id=1, replica_groups=mesh['dp'=8,'seq'=4] {'seq'}, use_global_device_ids=true, to_apply=%add.6 | all-reduce | flops 1152 | bytes 4608
  30.0 13.5 %all-gather.6.cloned.1.call-done = bf16[576,960]{1,0:T(8,128)(2,1)} async-done(((bf16[144,960]{1,0:T(8,128)(2,1)}), bf16[576,960]{1,0:T(8,128)(2,1)}) %all-gather.6.cloned.1.call-update) | async-done | bytes 1105936 | tf_op jit(solution)/shard_map/all_gather | solution.py:79
  43.5 3.1 fusion.45
  51.9 2.5 convert_element_type.162
  56.5 28.8 %all_gather.30 = bf16[576,576]{1,0:T(8,128)(2,1)} all-gather(bf16[144,576]{1,0:T(8,128)(2,1)S(1)} %convert_element_type.158), channel_id=1, replica_groups=mesh['dp'=8,'seq'=4] {'seq'}, dimensions={0}, use_global_device_ids=true | all-gather | bytes 829440 | tf_op jit(solution)/shard_map/all_gather | solution.py:80
  85.3 2.5 copy.119
  87.7 2.9 fusion.14
  93.9 3.0 all-gather.10.cloned.1.call-done
  98.7 15.4 %fusion.7 = (f32[3,3,512]{2,1,0:T(4,128)S(1)}, f32[3,2048,512,3]{2,1,3,0:T(8,128)}) fusion(pred[512,2048]{0,1:T(8,128)(4,1)S(1)} %copy-done.2, bf16[2048,3,64,1]{0,2,3,1:T(8,128)(2,1)S(1)} %bitcast.212, bf16[512,3,3,64]{0,3,2,1:T(8,128)(2,1)S(1)} %bitcast.220), kind=kOutput, calls=%fused_computation.17 | convolution fusion | flops 1236266496 | bytes 40192000 | tf_op jit(solution)/shard_map/qgjd,kgd->gjqk/dot_general | solution.py:137
  114.2 16.6 %exponential_reduce_fusion = f32[3,3,512]{2,1,0:T(4,128)S(1)} fusion(f32[3,2048,512,3]{2,1,3,0:T(8,128)} %get-tuple-element.172, f32[3,3,512]{2,1,0:T(4,128)S(1)} %get-tuple-element.171, pred[512,2048]{0,1:T(8,128)(4,1)S(1)} %copy-done.2), kind=kLoop, calls=%fused_computation.13 | loop fusion | flops 37744128 | bytes 38834176 | tf_op jit(solution)/shard_map/reduce_sum | solution.py:148
  130.8 15.8 %fusion.6 = (f32[3,3,512]{2,1,0:T(4,128)S(1)}, f32[3,2048,512,3]{2,1,3,0:T(8,128)}) fusion(pred[512,2048]{0,1:T(8,128)(4,1)S(1)} %get-tuple-element.167, bf16[2048,3,64,1]{0,2,3,1:T(8,128)(2,1)S(1)} %bitcast.210, bf16[512,3,3,64]{0,3,2,1:T(8,128)(2,1)S(1)} %bitcast.218), kind=kOutput, calls=%fused_computation.16 | convolution fusion | flops 1236266496 | bytes 40192000 | tf_op jit(solution)/shard_map/qgjd,kgd->gjqk/dot_general | solution.py:137
  146.6 16.6 %exponential_reduce_fusion.1 = f32[3,3,512]{2,1,0:T(4,128)S(1)} fusion(f32[3,2048,512,3]{2,1,3,0:T(8,128)} %get-tuple-element.174, f32[3,3,512]{2,1,0:T(4,128)S(1)} %get-tuple-element.173, pred[512,2048]{0,1:T(8,128)(4,1)S(1)} %get-tuple-element.167), kind=kLoop, calls=%fused_computation.15 | loop fusion | flops 37744128 | bytes 38834176 | tf_op jit(solution)/shard_map/reduce_sum | solution.py:148
  163.2 2.7 fusion.58
  165.9 18.3 %convolution_convert_fusion.5 = bf16[3,64,3,512]{3,1,2,0:T(8,128)(2,1)} fusion(bf16[2048,3,64,1]{0,2,3,1:T(8,128)(2,1)} %bitcast.230, f32[3,3,512]{2,1,0:T(4,128)S(1)} %log_add_fusion, f32[3,2048,512,3]{2,1,3,0:T(8,128)} %get-tuple-element.172, pred[512,2048]{0,1:T(8,128)(4,1)} %get-tuple-element.168), kind=kOutput, calls=%fused_computation.77 | convolution fusion | flops 1255440384 | bytes 40192000 | tf_op jit(solution)/shard_map/gjqk,kgd->qgjd/dot_general | solution.py:152
  184.2 17.4 %convolution_convert_fusion.6 = bf16[3,64,3,512]{3,1,2,0:T(8,128)(2,1)} fusion(bf16[2048,3,64,1]{0,2,3,1:T(8,128)(2,1)} %bitcast.232, f32[3,3,512]{2,1,0:T(4,128)S(1)} %log_add_fusion.1, f32[3,2048,512,3]{2,1,3,0:T(8,128)} %get-tuple-element.174, pred[512,2048]{0,1:T(8,128)(4,1)S(1)} %get-tuple-element.167), kind=kOutput, calls=%fused_computation.78 | convolution fusion | flops 1255440384 | bytes 40192000 | tf_op jit(solution)/shard_map/gjqk,kgd->qgjd/dot_general | solution.py:152
  201.6 4.0 multiply_reduce_fusion.4
  207.1 10.8 %fusion.46 = f32[1024,3072]{1,0:T(8,128)} fusion(bf16[576,3072]{1,0:T(8,128)(2,1)} %all-gather.12.cloned.1.call-done, f32[1024,576]{0,1:T(8,128)} %get-tuple-element.176, f32[576]{0:T(1024)S(1)} %convert_element_type.160, f32[1024]{0:T(1024)S(1)} %fusion.36), kind=kOutput, calls=%fused_computation.146 | convolution fusion | flops 3625648128 | bytes 18487552 | tf_op jit(solution)/shard_map/dot_general | solution.py:164
  217.9 30.4 %all-gather.14.cloned.1.call-done = bf16[1536,576]{0,1:T(8,128)(2,1)} async-done(((bf16[384,576]{0,1:T(8,128)(2,1)}), bf16[1536,576]{0,1:T(8,128)(2,1)}) %all-gather.14.cloned.1.call-update) | async-done | bytes 1769488 | tf_op jit(solution)/shard_map/all_gather | solution.py:83
  248.3 11.0 %fusion.30 = (f32[1024,1536]{1,0:T(8,128)S(1)}, f32[1024,1536]{1,0:T(8,128)}, bf16[1024,1536]{1,0:T(8,128)(2,1)}) fusion(f32[1024,3072]{1,0:T(8,128)} %fusion.46, bf16[1024,576]{0,1:T(8,128)(2,1)S(1)} %bitcast.206, bf16[1536,576]{0,1:T(8,128)(2,1)} %all-gather.14.cloned.1.call-done), kind=kOutput, calls=%fused_computation.98 | convolution fusion | flops 1833959424 | bytes 31260672 | tf_op jit(solution)/shard_map/td,fd->tf/dot_general | solution.py:178
  259.3 9.2 multiply_reduce_fusion
  271.8 31.8 %fusion.3 = (f32[3,3,512]{2,1,0:T(4,128)S(1)}, f32[3,2048,512,3]{2,1,3,0:T(8,128)}) fusion(f32[3,3,512]{2,1,0:T(4,128)S(1)} %log_add_fusion.1, f32[3,2048,512,3]{2,1,3,0:T(8,128)} %get-tuple-element.174, pred[512,2048]{0,1:T(8,128)(4,1)S(1)} %get-tuple-element.167, bf16[2048,3,64,1]{0,2,3,1:T(8,128)(2,1)} %bitcast.233, bf16[512,3,3,64]{0,3,2,1:T(8,128)(2,1)} %bitcast.240), kind=kOutput, calls=%fused_computation.7 | convolution fusion | flops 1264578048 | bytes 77959168 | tf_op jit(solution)/shard_map/qgjd,kgd->gjqk/dot_general | solution.py:207
  303.6 26.7 %fusion = (f32[3,3,512]{2,1,0:T(4,128)S(1)}, f32[3,2048,512,3]{2,1,3,0:T(8,128)}) fusion(f32[3,3,512]{2,1,0:T(4,128)S(1)} %log_add_fusion, f32[3,2048,512,3]{2,1,3,0:T(8,128)} %get-tuple-element.172, pred[512,2048]{0,1:T(8,128)(4,1)S(1)} %copy-done.3, bf16[2048,3,64,1]{0,2,3,1:T(8,128)(2,1)S(1)} %bitcast.231, bf16[512,3,3,64]{0,3,2,1:T(8,128)(2,1)} %bitcast.242), kind=kOutput, calls=%fused_computation.2 | convolution fusion | flops 1264578048 | bytes 77959168 | tf_op jit(solution)/shard_map/qgjd,kgd->gjqk/dot_general | solution.py:207
  330.3 61.6 %fusion.2 = (bf16[3,3,512,2048]{2,3,1,0:T(8,128)(2,1)}, bf16[3,3,512,2048]{2,3,1,0:T(8,128)(2,1)}) fusion(f32[3,2048,512,3]{2,1,3,0:T(8,128)} %get-tuple-element.179, f32[3,3,512]{2,1,0:T(4,128)S(1)} %get-tuple-element.178, f32[3,3,512]{2,1,0:T(4,128)S(1)} %log_add_fusion, f32[3,2048,512,3]{2,1,3,0:T(8,128)} %get-tuple-element.172, ...), kind=kLoop, calls=%fused_computation.4 | loop fusion | flops 132120576 | bytes 190914560 | tf_op jit(solution)/shard_map/convert_element_type | solution.py:217
  392.0 12.3 %fusion.20 = bf16[3,64,2048]{2,1,0:T(8,128)(2,1)S(1)} fusion(bf16[512,3,3,64]{0,3,2,1:T(8,128)(2,1)} %bitcast.219, bf16[3,3,512,2048]{2,3,1,0:T(8,128)(2,1)} %get-tuple-element.183), kind=kOutput, calls=%fused_computation.48 | convolution fusion | flops 1208745984 | bytes 20250624 | tf_op jit(solution)/shard_map/gjqk,qgjd->kgd/dot_general | solution.py:226
  404.3 13.2 %fusion.19 = bf16[3,64,2048]{2,1,0:T(8,128)(2,1)} fusion(bf16[512,3,3,64]{0,3,2,1:T(8,128)(2,1)} %bitcast.217, bf16[3,3,512,2048]{2,3,1,0:T(8,128)(2,1)} %get-tuple-element.184), kind=kOutput, calls=%fused_computation.47 | convolution fusion | flops 1208745984 | bytes 20250624 | tf_op jit(solution)/shard_map/gjqk,qgjd->kgd/dot_general | solution.py:226
  420.0 17.2 %fusion.18 = bf16[3,64,2048]{2,1,0:T(8,128)(2,1)S(1)} fusion(bf16[512,3,3,64]{0,3,2,1:T(8,128)(2,1)} %bitcast.243, f32[3,3,512]{2,1,0:T(4,128)S(1)} %log_add_fusion, f32[3,2048,512,3]{2,1,3,0:T(8,128)} %get-tuple-element.172, pred[512,2048]{0,1:T(8,128)(4,1)S(1)} %copy-done.3), kind=kOutput, calls=%fused_computation.46 | convolution fusion | flops 1255538688 | bytes 40192000 | tf_op jit(solution)/shard_map/gjqk,qgjd->kgd/dot_general | solution.py:211
  438.5 17.3 %fusion.17 = bf16[3,64,2048]{2,1,0:T(8,128)(2,1)S(1)} fusion(bf16[512,3,3,64]{0,3,2,1:T(8,128)(2,1)} %bitcast.241, f32[3,3,512]{2,1,0:T(4,128)S(1)} %log_add_fusion.1, f32[3,2048,512,3]{2,1,3,0:T(8,128)} %get-tuple-element.174, pred[512,2048]{0,1:T(8,128)(4,1)S(1)} %get-tuple-element.167), kind=kOutput, calls=%fused_computation.45 | convolution fusion | flops 1255538688 | bytes 40192000 | tf_op jit(solution)/shard_map/gjqk,qgjd->kgd/dot_general | solution.py:211
  457.0 3.6 pad_maximum_fusion.2
  460.6 72.0 %copy.111 = bf16[2,2048,192]{0,2,1:T(8,128)(2,1)} copy(bf16[2,2048,192]{1,0,2:T(2,128)(2,1)S(1)} %pad_maximum_fusion.2) | data formatting | bytes 3145728
  532.7 135.4 %reshape.399 = bf16[2048,384]{1,0:T(8,128)(2,1)} reshape(bf16[2048,192,2]{2,1,0:T(8,128)(2,1)} %bitcast.60) | data formatting | bytes 3145728
  668.1 5.1 convolution_convert_fusion.1
  673.2 4.1 copy.113
  677.4 3.3 convolution_convert_fusion.4
  680.7 8.2 convolution_multiply_fusion
  689.0 8.3 convolution_multiply_fusion.1
  702.3 55.1 %reshape.400 = bf16[512,192,2]{2,1,0:T(8,128)(2,1)} reshape(bf16[512,384]{1,0:T(8,128)(2,1)} %reduce-scatter.19.cloned.1.call-done) | data formatting | bytes 786432
  757.4 23.6 %copy.112 = bf16[2,512,192]{1,0,2:T(2,128)(2,1)} copy(bf16[2,512,192]{0,2,1:T(8,128)(2,1)} %bitcast.197) | data formatting | bytes 786432
  783.1 2.4 convolution_convert_fusion.2
  785.6 11.0 %convolution_convert_fusion = bf16[576,3072]{1,0:T(8,128)(2,1)} fusion(f32[1024,1536]{1,0:T(8,128)} %get-tuple-element.143, f32[1024,1536]{1,0:T(8,128)} %copy-done.64, f32[1024,576]{0,1:T(8,128)} %get-tuple-element.176, f32[576]{0:T(1024)S(1)} %copy-done.51, f32[1024]{0:T(1024)S(1)} %copy-done.53), kind=kOutput, calls=%fused_computation.27 | convolution fusion | flops 3633709056 | bytes 18487552 | tf_op jit(solution)/shard_map/td,tf->df/dot_general | solution.py:181
  797.6 5.3 add_convert_fusion.2
  804.7 3.0 multiply_reduce_fusion.1
  809.7 4.1 reduce-scatter.13.cloned.1.call-done
  813.9 67.4 %reduce-scatter.17.cloned.1.call-done = bf16[144,3072]{1,0:T(8,128)(2,1)} async-done(((bf16[576,3072]{1,0:T(8,128)(2,1)}), bf16[144,3072]{1,0:T(8,128)(2,1)}) %reduce-scatter.17.cloned.1.call-update) | async-done | bytes 884752 | tf_op jit(solution)/shard_map/reduce_scatter | solution.py:272
  881.3 2.9 fusion.24
  885.5 10.8 %all-reduce.12 = (bf16[576]{0:T(1024)(128)(2,1)S(1)}, bf16[576]{0:T(1024)(128)(2,1)S(1)}) all-reduce(bf16[576]{0:T(1024)(128)(2,1)S(1)} %get-tuple-element.106, bf16[576]{0:T(1024)(128)(2,1)S(1)} %copy-done.55), channel_id=4, replica_groups=mesh['dp'=8,'seq'=4] {'seq'}, use_global_device_ids=true, to_apply=%region_13.14.clone | all-reduce | flops 1152 | bytes 4608
  896.5 11.9 %all-reduce.10 = (bf16[144]{0:T(256)(128)(2,1)S(1)}, bf16[144]{0:T(256)(128)(2,1)S(1)}) all-reduce(bf16[144]{0:T(256)(128)(2,1)S(1)} %dynamic-slice.3, bf16[144]{0:T(256)(128)(2,1)S(1)} %dynamic-slice.5), channel_id=1, replica_groups=mesh['dp'=8,'seq'=4] {'dp'}, use_global_device_ids=true, to_apply=%region_14.15 | all-reduce | flops 288 | bytes 1152 | tf_op jit(solution)/shard_map/psum | solution.py:280
  909.6 36.8 %all-reduce.16.cloned.1.call-done = (bf16[144,960]{1,0:T(8,128)(2,1)}, bf16[144,576]{1,0:T(8,128)(2,1)}, bf16[144,3072]{1,0:T(8,128)(2,1)}, bf16[384,576]{0,1:T(8,128)(2,1)}) async-done(((bf16[144,960]{1,0:T(8,128)(2,1)}, bf16[144,576]{1,0:T(8,128)(2,1)}, bf16[144,3072]{1,0:T(8,128)(2,1)}, bf16[384,576]{0,1:T(8,128)(2,1)}), (bf16[144,960]{1,0:T(8,128)(2,1)}, bf16[144,576]{1,0:T(8,128)(2,1)}, ...) | async-done | bytes 1769488 | tf_op jit(solution)/shard_map/psum | solution.py:281
  955.2 3.5 multiply_subtract_fusion
  (224 shorter events, 53.1 us)
Async XLA Ops:
  7.2 21.6 %copy-start.11 = (bf16[2,512,576]{1,2,0:T(8,128)(2,1)S(1)}, bf16[2,512,576]{1,2,0:T(8,128)(2,1)}, u32[]{:S(2)}) copy-start(bf16[2,512,576]{1,2,0:T(8,128)(2,1)} %param.21) | copy-start | bytes 3538948
  7.2 21.5 %copy-start.54 = (s32[2,512]{1,0:T(2,128)S(1)}, s32[2,512]{1,0:T(2,128)}, u32[]{:S(2)}) copy-start(s32[2,512]{1,0:T(2,128)} %param.22) | copy-start | bytes 12292
  7.2 36.3 %all-gather.6.cloned.1.call-start = ((), (), s32[]{:S(2)}) async-start(), calls=%async_computation.6 | async-start | bytes 1474560 | tf_op jit(solution)/shard_map/all_gather | solution.py:79
  9.2 87.7 %all-gather.10.cloned.1.call-start = ((), (), s32[]{:S(2)}) async-start(), calls=%async_computation.8 | async-start | bytes 1966080 | tf_op jit(solution)/shard_map/all_gather | solution.py:123
  26.6 16.9 %copy-start.46 = (f32[576]{0:T(1024)}, f32[576]{0:T(1024)S(1)}, u32[]{:S(2)}) copy-start(f32[576]{0:T(1024)S(1)} %convert_element_type.150) | copy-start | bytes 6916
  28.7 14.8 %copy-start.48 = (f32[1024]{0:T(1024)}, f32[1024]{0:T(1024)S(1)}, u32[]{:S(2)}) copy-start(f32[1024]{0:T(1024)S(1)} %rsqrt.20) | copy-start | bytes 12292
  29.4 172.2 %copy-start = (f32[2,72,8,512]{3,2,0,1:T(8,128)}, f32[2,72,8,512]{3,2,0,1:T(8,128)S(1)}, u32[]{:S(2)}) copy-start(f32[2,72,8,512]{3,2,0,1:T(8,128)S(1)} %copy.118) | copy-start | bytes 7077892
  29.9 18.7 %copy-start.16 = (f32[1024,32]{0,1:T(8,128)}, f32[1024,32]{0,1:T(8,128)S(1)}, u32[]{:S(2)}) copy-start(f32[1024,32]{0,1:T(8,128)S(1)} %get-tuple-element.162) | copy-start | bytes 393220
  29.9 60.7 %copy-start.14 = (f32[1024,32]{0,1:T(8,128)}, f32[1024,32]{0,1:T(8,128)S(1)}, u32[]{:S(2)}) copy-start(f32[1024,32]{0,1:T(8,128)S(1)} %get-tuple-element.161) | copy-start | bytes 393220
  49.9 113.4 %all-gather.8.cloned.1.call-start = ((), (), s32[]{:S(2)}) async-start(), calls=%async_computation.7 | async-start | bytes 1966080 | tf_op jit(solution)/shard_map/all_gather | solution.py:124
  51.9 155.2 %all-gather.12.cloned.1.call-start = ((), (), s32[]{:S(2)}) async-start(), calls=%async_computation.9 | async-start | bytes 4423680 | tf_op jit(solution)/shard_map/all_gather | solution.py:82
  54.5 193.8 %all-gather.14.cloned.1.call-start = ((), (), s32[]{:S(2)}) async-start(), calls=%async_computation.10 | async-start | bytes 2211840 | tf_op jit(solution)/shard_map/all_gather | solution.py:83
  55.4 643.5 %reduce-scatter.11.cloned.1.call-start = ((), (), s32[]{:S(2)}) async-start(), calls=%async_computation.11 | async-start | bytes 1966080 | tf_op jit(solution)/shard_map/reduce_scatter | solution.py:231
  55.4 213.1 %copy-start.50 = (f32[576]{0:T(1024)}, f32[576]{0:T(1024)S(1)}, u32[]{:S(2)}) copy-start(f32[576]{0:T(1024)S(1)} %convert_element_type.160) | copy-start | bytes 6916
  98.5 15.6 %copy-start.21 = (bf16[1,2048,192]{1,2,0:T(8,128)(2,1)}, bf16[1,2048,192]{1,2,0:T(8,128)(2,1)S(1)}, u32[]{:S(2)}) copy-start(bf16[1,2048,192]{1,2,0:T(8,128)(2,1)S(1)} %get-tuple-element.150) | copy-start | bytes 2359300
  98.6 32.2 %copy-start.19 = (bf16[1,2048,192]{1,2,0:T(8,128)(2,1)}, bf16[1,2048,192]{1,2,0:T(8,128)(2,1)S(1)}, u32[]{:S(2)}) copy-start(bf16[1,2048,192]{1,2,0:T(8,128)(2,1)S(1)} %get-tuple-element.149) | copy-start | bytes 2359300
  114.2 16.6 %copy-start.25 = (bf16[512,9,64]{0,2,1:T(8,128)(2,1)S(1)}, bf16[512,9,64]{0,2,1:T(8,128)(2,1)}, u32[]{:S(2)}) copy-start(bf16[512,9,64]{0,2,1:T(8,128)(2,1)} %get-tuple-element.155) | copy-start | bytes 1769476
  205.6 62.9 %copy-start.52 = (f32[1024]{0:T(1024)}, f32[1024]{0:T(1024)S(1)}, u32[]{:S(2)}) copy-start(f32[1024]{0:T(1024)S(1)} %fusion.36) | copy-start | bytes 12292
  207.1 41.2 %copy-start.9 = (bf16[2,72,8,512]{3,2,0,1:T(8,128)(2,1)S(1)}, bf16[2,72,8,512]{3,2,0,1:T(8,128)(2,1)}, u32[]{:S(2)}) copy-start(bf16[2,72,8,512]{3,2,0,1:T(8,128)(2,1)} %copy.119) | copy-start | bytes 3538948
  248.3 11.0 %copy-start.7 = (f32[1024,576]{0,1:T(8,128)S(1)}, f32[1024,576]{0,1:T(8,128)}, u32[]{:S(2)}) copy-start(f32[1024,576]{0,1:T(8,128)} %get-tuple-element.176) | copy-start | bytes 7077892
  248.3 11.0 %copy-start.62 = (bf16[576,3072]{1,0:T(8,128)(2,1)S(1)}, bf16[576,3072]{1,0:T(8,128)(2,1)}, u32[]{:S(2)}) copy-start(bf16[576,3072]{1,0:T(8,128)(2,1)} %all-gather.12.cloned.1.call-done) | copy-start | bytes 10616836
  259.3 9.2 copy-start.64
  271.8 31.8 %copy-start.3 = (pred[512,2048]{0,1:T(8,128)(4,1)S(1)}, pred[512,2048]{0,1:T(8,128)(4,1)}, u32[]{:S(2)}) copy-start(pred[512,2048]{0,1:T(8,128)(4,1)} %get-tuple-element.168) | copy-start | bytes 3145732
  271.8 31.8 %copy-start.35 = (bf16[1,2048,192]{1,2,0:T(8,128)(2,1)S(1)}, bf16[1,2048,192]{1,2,0:T(8,128)(2,1)}, u32[]{:S(2)}) copy-start(bf16[1,2048,192]{1,2,0:T(8,128)(2,1)} %get-tuple-element.152) | copy-start | bytes 2359300
  419.9 282.4 %reduce-scatter.19.cloned.1.call-start = ((), (), s32[]{:S(2)}) async-start(), calls=%async_computation.15 | async-start | bytes 1966080
  532.7 135.4 %copy-start.10 = (bf16[2,72,8,512]{3,2,0,1:T(8,128)(2,1)S(1)}, bf16[2,72,8,512]{3,2,0,1:T(8,128)(2,1)}, u32[]{:S(2)}) copy-start(bf16[2,72,8,512]{3,2,0,1:T(8,128)(2,1)} %copy.119) | copy-start | bytes 3538948
  668.1 139.7 %reduce-scatter.21.cloned.1.call-start = ((), (), s32[]{:S(2)}) async-start(), calls=%async_computation.16 | async-start | bytes 2457600
  677.3 132.4 %reduce-scatter.15.cloned.1.call-start = ((), (), s32[]{:S(2)}) async-start(), calls=%async_computation.13 | async-start | bytes 921600 | tf_op jit(solution)/shard_map/reduce_scatter | solution.py:266
  680.7 8.3 copy-start.20
  688.9 8.4 copy-start.15
  688.9 8.4 copy-start.18
  688.9 125.0 %reduce-scatter.13.cloned.1.call-start = ((), (), s32[]{:S(2)}) async-start(), calls=%async_computation.12 | async-start | bytes 1474560 | tf_op jit(solution)/shard_map/reduce_scatter | solution.py:263
  785.5 95.7 %reduce-scatter.17.cloned.1.call-start = ((), (), s32[]{:S(2)}) async-start(), calls=%async_computation.14 | async-start | bytes 4423680 | tf_op jit(solution)/shard_map/reduce_scatter | solution.py:272
  796.7 149.7 %all-reduce.16.cloned.1.call-start = ((), (), s32[]{:S(2)}) async-start(), calls=%async_computation.17 | async-start | bytes 3612672 | tf_op jit(solution)/shard_map/psum | solution.py:281
  797.6 6.4 copy-start.63
  807.8 73.5 %copy-start.45 = (f32[1,4,2,128]{3,1,2,0:T(4,128)S(1)}, f32[1,4,2,128]{3,1,2,0:T(4,128)}, u32[]{:S(2)}) copy-start(f32[1,4,2,128]{3,1,2,0:T(4,128)} %copy-done.44) | copy-start | bytes 12292
  884.3 24.1 %copy-start.56 = (f32[144]{0:T(256)S(1)}, f32[144]{0:T(256)}, u32[]{:S(2)}) copy-start(f32[144]{0:T(256)} %param.24) | copy-start | bytes 1732
  884.3 24.1 %copy-start.57 = (f32[144]{0:T(256)S(1)}, f32[144]{0:T(256)}, u32[]{:S(2)}) copy-start(f32[144]{0:T(256)} %param.30) | copy-start | bytes 1732
  884.3 24.1 %copy-start.58 = (f32[144]{0:T(256)S(1)}, f32[144]{0:T(256)}, u32[]{:S(2)}) copy-start(f32[144]{0:T(256)} %param.36) | copy-start | bytes 1732
  884.3 24.7 %copy-start.59 = (f32[144]{0:T(256)S(1)}, f32[144]{0:T(256)}, u32[]{:S(2)}) copy-start(f32[144]{0:T(256)} %param.27) | copy-start | bytes 1732
  884.3 24.7 %copy-start.60 = (f32[144]{0:T(256)S(1)}, f32[144]{0:T(256)}, u32[]{:S(2)}) copy-start(f32[144]{0:T(256)} %param.33) | copy-start | bytes 1732
  884.4 24.6 %copy-start.61 = (f32[144]{0:T(256)S(1)}, f32[144]{0:T(256)}, u32[]{:S(2)}) copy-start(f32[144]{0:T(256)} %param.39) | copy-start | bytes 1732
  884.4 62.0 %copy-start.29 = (f32[144,576]{1,0:T(8,128)S(1)}, f32[144,576]{1,0:T(8,128)}, u32[]{:S(2)}) copy-start(f32[144,576]{1,0:T(8,128)} %param.26) | copy-start | bytes 995332
  884.4 62.0 %copy-start.41 = (f32[144,576]{1,0:T(8,128)S(1)}, f32[144,576]{1,0:T(8,128)}, u32[]{:S(2)}) copy-start(f32[144,576]{1,0:T(8,128)} %param.32) | copy-start | bytes 995332
  884.4 62.0 %copy-start.42 = (f32[144,576]{1,0:T(8,128)S(1)}, f32[144,576]{1,0:T(8,128)}, u32[]{:S(2)}) copy-start(f32[144,576]{1,0:T(8,128)} %param.38) | copy-start | bytes 995332
  884.4 64.2 %copy-start.24 = (f32[144,960]{1,0:T(8,128)S(1)}, f32[144,960]{1,0:T(8,128)}, u32[]{:S(2)}) copy-start(f32[144,960]{1,0:T(8,128)} %param.25) | copy-start | bytes 1658884
  884.4 64.1 %copy-start.36 = (f32[144,960]{1,0:T(8,128)S(1)}, f32[144,960]{1,0:T(8,128)}, u32[]{:S(2)}) copy-start(f32[144,960]{1,0:T(8,128)} %param.31) | copy-start | bytes 1658884
  884.4 64.1 %copy-start.37 = (f32[144,960]{1,0:T(8,128)S(1)}, f32[144,960]{1,0:T(8,128)}, u32[]{:S(2)}) copy-start(f32[144,960]{1,0:T(8,128)} %param.37) | copy-start | bytes 1658884
  (30 other events, 67.0 us)
Sparse Core Ops, SparseCore 0:
  10.2 33.2 all-gather.5
  50.0 46.8 all-gather.9
  99.0 37.1 all-gather.7
  138.2 68.8 all-gather.11
  209.1 39.1 all-gather.13
  420.1 34.0 reduce-scatter.10
  668.2 34.0 reduce-scatter.18
  704.6 40.3 reduce-scatter.20
  747.9 22.1 reduce-scatter.14
  785.7 28.1 reduce-scatter.12
  816.2 65.0 reduce-scatter.16
  885.4 60.9 all-reduce.15
where the time goes:
time: 972 us; the launch traced here: 966 us
  local copies, waits for them, and re-layouts  323 us (33%)
  matrix products  271 us (28%)
  waiting for transfers between devices  158 us (16%)
  other arithmetic  131 us (13%)
  blocking collectives  65 us (7%)
  between operations  16.7 us (2%)
    unnamed x146, local copies, waits for them, and re-layouts  303 us
    reduce_scatter x1, waiting for transfers between devices, on_device(): lax.psum_scatter(grads[4].astype(jnp.bfloat16), 'seq', scatter_dimension=...  67.4 us
    convert_element_type x1, other arithmetic, on_device(): score_grad = (probs * (prob_grad - jnp.sum(probs * prob_grad, axis=-1, ke...  61.6 us
    dot_general x2, matrix products, on_device(): jnp.einsum('qgjd,kgd->gjqk', heads_grad[number], value_heads, preferred_e...  58.5 us
    psum x1, waiting for transfers between devices, on_device(): lax.psum(slices[1].astype(jnp.bfloat16), 'dp').astype(jnp.float32)  36.8 us
    dot_general x2, matrix products, on_device(): jnp.einsum('gjqk,kgd->qgjd', probs.astype(jnp.bfloat16), value_heads, pre...  35.7 us
    dot_general x2, matrix products, on_device(): jnp.einsum('gjqk,qgjd->kgd', probs_low, heads_grad[number], preferred_ele...  34.5 us
    reduce_sum x2, other arithmetic, on_device(): jnp.sum(jnp.exp(masked - top_score), axis=-1, keepdims=True)  33.1 us
  transfers between devices with their start and end apart: 12, of which 8 were waited for; matrix products, arithmetic and copies ran while one was open for 55% of the time, Pallas kernels for 0%

commit v1 on v0

v1 whole, which is shorter than its diff:
```python
import functools

import jax
import jax.numpy as jnp
from jax import lax
from jax.experimental import pallas as pl
from jax.experimental.pallas import tpu as pltpu
from jax.sharding import PartitionSpec as P

HEADS = 9
KV_HEADS = 3
HEAD_DIM = 64
HALF = HEAD_DIM // 2
GROUP = HEADS // KV_HEADS
STEP = 2

norm_eps = 1e-05
rope_base = 100000.0
beta_one = 0.9
beta_two = 0.95
adam_eps = 1e-08
learn_rate = 0.2
decay_rate = 0.1

bf16 = jnp.bfloat16
f32 = jnp.float32
NEG = -1e30
NN = (((1,), (0,)), ((), ()))
NT = (((1,), (1,)), ((), ()))
MESH = pl.DeviceIdType.MESH
VMEM = pl.BlockSpec(memory_space=pltpu.VMEM)
HBM = pl.BlockSpec(memory_space=pl.ANY)


def dot(left, right, dims=NN):
    return lax.dot_general(left, right, dims, preferred_element_type=f32)


def place():
    dp = lax.axis_index("dp")
    base = (dp // 8) * 8
    chip = (dp % 8) // 2
    core = dp % 2
    return base, chip, core, lax.axis_index("seq")


def gather_kernel(count, blocks, *refs):
    quarters = refs[:count]
    fulls = refs[count : 2 * count]
    local_sem, send_sem, recv_sem = refs[2 * count :]
    base, chip, core, z = place()

    def window(number, which, quarter):
        kind, size, rows = blocks[number]
        if kind == "cols":
            return (
                pl.ds(pl.multiple_of(quarter * rows, 16), rows),
                pl.ds(pl.multiple_of(which * size, 128), size),
            )
        return (pl.ds(pl.multiple_of(quarter * rows + which * size, 16), size), slice(None))

    def dev(p, c, zz):
        return {"dp": base + 2 * p + c, "seq": zz}

    barrier = pltpu.get_barrier_semaphore()
    for r in range(1, 4):
        pl.semaphore_signal(
            barrier, inc=1, device_id=dev(chip, core, (z + r) % 4), device_id_type=MESH
        )
        pl.semaphore_signal(
            barrier, inc=1, device_id=dev((chip + r) % 4, core, z), device_id_type=MESH
        )
    pl.semaphore_signal(barrier, inc=1, device_id=dev(chip, 1 - core, z), device_id_type=MESH)
    pl.semaphore_wait(barrier, 7)

    def copy(number, src, dst, slot, target):
        return pltpu.make_async_remote_copy(
            src_ref=src,
            dst_ref=dst,
            send_sem=send_sem.at[number, slot],
            recv_sem=recv_sem.at[number, slot],
            device_id=target,
            device_id_type=MESH,
        )

    mine = 2 * chip + core
    started = []
    for number in range(count):
        for r in range(1, 4):
            started.append(
                copy(
                    number,
                    quarters[number].at[window(number, mine, 0)],
                    fulls[number].at[window(number, mine, z)],
                    r - 1,
                    dev(chip, core, (z + r) % 4),
                )
            )
            started[-1].start()
    locals_ = []
    for number in range(count):
        rows = quarters[number].shape[0]
        own = pltpu.make_async_copy(
            quarters[number],
            fulls[number].at[pl.ds(pl.multiple_of(z * rows, 16), rows), :],
            local_sem.at[number],
        )
        own.start()
        locals_.append(own)

    def landed(number, which, quarter, slot):
        ref = fulls[number].at[window(number, which, quarter)]
        return copy(number, ref, ref, slot, dev(chip, 1 - core, z))

    for number in range(count):
        for r in range(1, 4):
            quarter = (z + 4 - r) % 4
            landed(number, mine, quarter, r - 1).wait_recv()
            ref = fulls[number].at[window(number, mine, quarter)]
            for s in range(1, 4):
                started.append(
                    copy(number, ref, ref, 3 + 3 * (r - 1) + s - 1, dev((chip + s) % 4, core, z))
                )
                started[-1].start()
            started.append(copy(number, ref, ref, 12 + r - 1, dev(chip, 1 - core, z)))
            started[-1].start()
    for number in range(count):
        for r in range(1, 4):
            quarter = (z + 4 - r) % 4
            for s in range(1, 4):
                which = 2 * ((chip + 4 - s) % 4) + core
                landed(number, which, quarter, 3 + 3 * (r - 1) + s - 1).wait_recv()
                ref = fulls[number].at[window(number, which, quarter)]
                started.append(
                    copy(number, ref, ref, 15 + 3 * (r - 1) + s - 1, dev(chip, 1 - core, z))
                )
                started[-1].start()
    for number in range(count):
        for r in range(1, 4):
            quarter = (z + 4 - r) % 4
            landed(number, 2 * chip + 1 - core, quarter, 12 + r - 1).wait_recv()
            for s in range(1, 4):
                which = 2 * ((chip + 4 - s) % 4) + 1 - core
                landed(number, which, quarter, 15 + 3 * (r - 1) + s - 1).wait_recv()
    for item in started:
        item.wait_send()
    for item in locals_:
        item.wait()


def block_kind(array, row_blocks):
    if row_blocks:
        return ("rows", array.shape[0] // 8, array.shape[0])
    return ("cols", array.shape[1] // 8, array.shape[0])


def gather_weights(arrays, by_rows, collective):
    count = len(arrays)
    blocks = tuple(block_kind(a, r) for a, r in zip(arrays, by_rows))
    return pl.pallas_call(
        functools.partial(gather_kernel, count, blocks),
        out_shape=[jax.ShapeDtypeStruct((4 * a.shape[0], a.shape[1]), bf16) for a in arrays],
        in_specs=[HBM] * count,
        out_specs=[HBM] * count,
        scratch_shapes=[
            pltpu.SemaphoreType.DMA((count,)),
            pltpu.SemaphoreType.DMA((count, 24)),
            pltpu.SemaphoreType.DMA((count, 24)),
        ],
        compiler_params=pltpu.CompilerParams(collective_id=collective, has_side_effects=True),
    )(*arrays)


def scatter_kernel(count, blocks, *refs):
    grads = refs[:count]
    outs = refs[count : 2 * count]
    rest = refs[2 * count :]
    r0s = rest[:count]
    s0s = rest[count : 2 * count]
    r1s = rest[2 * count : 3 * count]
    r2s = rest[3 * count : 4 * count]
    send_sem, recv_sem = rest[4 * count :]
    base, chip, core, z = place()

    def dev(p, c, zz):
        return {"dp": base + 2 * p + c, "seq": zz}

    barrier = pltpu.get_barrier_semaphore()
    for r in range(1, 4):
        pl.semaphore_signal(
            barrier, inc=1, device_id=dev(chip, core, (z + r) % 4), device_id_type=MESH
        )
        pl.semaphore_signal(
            barrier, inc=1, device_id=dev((chip + r) % 4, core, z), device_id_type=MESH
        )
    pl.semaphore_signal(barrier, inc=1, device_id=dev(chip, 1 - core, z), device_id_type=MESH)
    pl.semaphore_wait(barrier, 7)

    started = []

    def copy(number, src, dst, slot, target):
        return pltpu.make_async_remote_copy(
            src_ref=src,
            dst_ref=dst,
            send_sem=send_sem.at[number, slot],
            recv_sem=recv_sem.at[number, slot],
            device_id=target,
            device_id_type=MESH,
        )

    def send(number, src, dst, slot, target):
        item = copy(number, src, dst, slot, target)
        item.start()
        started.append(item)

    def await_(number, ref, slot):
        copy(number, ref, ref, slot, dev(chip, 1 - core, z)).wait_recv()

    def block_of(number, which):
        kind, size, rows = blocks[number]
        if kind == "cols":
            return (slice(None), slice(None), pl.ds(pl.multiple_of(which * size, 128), size))
        return (slice(None), pl.ds(pl.multiple_of(which * size, 16), size), slice(None))

    def out_block(number, which):
        return block_of(number, which)[1:]

    for number in range(count):
        for s in range(4):
            p = (chip + s) % 4
            send(
                number,
                grads[number].at[block_of(number, 2 * p + 1 - core)],
                r0s[number].at[s],
                s,
                dev(chip, 1 - core, z),
            )
    for number in range(count):
        for s in (1, 2, 3, 0):
            p = (chip + s) % 4
            await_(number, r0s[number].at[s], s)
            total = (
                grads[number][block_of(number, 2 * p + core)].astype(f32)
                + r0s[number][s].astype(f32)
            )
            s0s[number][s] = total.astype(bf16)
            if s > 0:
                send(
                    number, s0s[number].at[s], r1s[number].at[s - 1], 3 + s, dev(p, core, z)
                )
    for number in range(count):
        total = s0s[number][0].astype(f32)
        for s in range(1, 4):
            await_(number, r1s[number].at[s - 1], 3 + s)
            total = total + r1s[number][s - 1].astype(f32)
        s0s[number][0] = total.astype(bf16)
        for r in range(1, 4):
            send(
                number,
                s0s[number].at[0, (z + r) % 4],
                r2s[number].at[r - 1],
                6 + r,
                dev(chip, core, (z + r) % 4),
            )
    mine = 2 * chip + core
    for number in range(count):
        total = s0s[number][0, z].astype(f32)
        for r in range(1, 4):
            await_(number, r2s[number].at[r - 1], 6 + r)
            total = total + r2s[number][r - 1].astype(f32)
        ref = outs[number].at[out_block(number, mine)]
        outs[number][out_block(number, mine)] = total.astype(bf16)
        for s in range(1, 4):
            send(number, ref, ref, 9 + s, dev((chip + s) % 4, core, z))
        send(number, ref, ref, 13, dev(chip, 1 - core, z))
    for number in range(count):
        for s in range(1, 4):
            which = 2 * ((chip + 4 - s) % 4) + core
            ref = outs[number].at[out_block(number, which)]
            await_(number, ref, 9 + s)
            send(number, ref, ref, 13 + s, dev(chip, 1 - core, z))
    for number in range(count):
        await_(number, outs[number].at[out_block(number, 2 * chip + 1 - core)], 13)
        for s in range(1, 4):
            which = 2 * ((chip + 4 - s) % 4) + 1 - core
            await_(number, outs[number].at[out_block(number, which)], 13 + s)
    for item in started:
        item.wait_send()


def scatter_grads(arrays, by_rows, collective):
    count = len(arrays)
    split = [a.reshape(4, a.shape[0] // 4, a.shape[1]) for a in arrays]
    blocks = tuple(block_kind(a[0], r) for a, r in zip(split, by_rows))
    parts = []
    for array, (kind, size, rows) in zip(split, blocks):
        parts.append((4, rows, size) if kind == "cols" else (4, size, array.shape[2]))
    scratch = (
        [pltpu.VMEM((4,) + part, bf16) for part in parts]
        + [pltpu.VMEM((4,) + part, bf16) for part in parts]
        + [pltpu.VMEM((3,) + part, bf16) for part in parts]
        + [pltpu.VMEM((3,) + part[1:], bf16) for part in parts]
    )
    return pl.pallas_call(
        functools.partial(scatter_kernel, count, blocks),
        out_shape=[jax.ShapeDtypeStruct(a.shape[1:], bf16) for a in split],
        in_specs=[VMEM] * count,
        out_specs=[VMEM] * count,
        scratch_shapes=scratch
        + [pltpu.SemaphoreType.DMA((count, 17)), pltpu.SemaphoreType.DMA((count, 17))],
        compiler_params=pltpu.CompilerParams(
            collective_id=collective, has_side_effects=True, vmem_limit_bytes=60 << 20
        ),
    )(*split)


def column_row(tile, lane, height):
    return tile.astype(f32).T[lane : lane + 1, :]


def qkv_kernel(inner, x_ref, w_ref, cos_ref, sin_ref, q_ref, kv_ref):
    model = x_ref.shape[2]
    width = inner + 2 * KV_HEADS * HEAD_DIM
    tile = width // 128 * 128
    gain = column_row(w_ref[:, tile : tile + 128], width - tile, model)
    w_t = w_ref[...].T[:width, :]
    for s in range(2):
        x = x_ref[s].astype(f32)
        rho = lax.rsqrt(jnp.mean(x * x, axis=1, keepdims=True) + norm_eps)
        a = (x * rho * gain).astype(bf16)
        z = dot(w_t, a, NT)
        cos = cos_ref[s]
        sin = sin_ref[s]

        def rotated(head):
            u1 = z[head * HEAD_DIM : head * HEAD_DIM + HALF]
            u2 = z[head * HEAD_DIM + HALF : (head + 1) * HEAD_DIM]
            return jnp.concatenate([u1 * cos - u2 * sin, u2 * cos + u1 * sin], axis=0).astype(bf16)

        for head in range(HEADS):
            q_ref[s, head] = rotated(head) * jnp.asarray(0.125, bf16)
        for head in range(KV_HEADS):
            kv_ref[s, head] = rotated(HEADS + head)
            low = inner + (KV_HEADS + head) * HEAD_DIM
            kv_ref[s, KV_HEADS + head] = z[low : low + HEAD_DIM].astype(bf16)


def project(x, w, cos, sin):
    chunk = x.shape[1]
    return pl.pallas_call(
        functools.partial(qkv_kernel, HEADS * HEAD_DIM),
        out_shape=[
            jax.ShapeDtypeStruct((2, HEADS, HEAD_DIM, chunk), bf16),
            jax.ShapeDtypeStruct((2, 2 * KV_HEADS, HEAD_DIM, chunk), bf16),
        ],
        in_specs=[VMEM] * 4,
        out_specs=[VMEM] * 2,
        compiler_params=pltpu.CompilerParams(vmem_limit_bytes=56 << 20),
    )(x, w, cos, sin)


def order_kv(core, own_ref, other_ref, ordered):
    for core_is in range(2):

        @pl.when(core == core_is)
        def _():
            ordered[core_is] = own_ref[0]
            ordered[3 - core_is] = own_ref[1]
            ordered[1 - core_is] = other_ref[0]
            ordered[2 + core_is] = other_ref[1]


def visible(chunk, key_start, keys, lows, first_query, own, causal):
    size = lows.shape[1]
    shape = (keys, size - first_query)
    key = lax.broadcasted_iota(jnp.int32, shape, 0) + key_start
    seen = key >= lows[:, first_query:]
    if causal:
        query = lax.broadcasted_iota(jnp.int32, shape, 1) + (own + first_query)
        seen = seen & (key <= query)
    return seen


def forward_kernel(q_ref, own_ref, other_ref, low_ref, o_ref, lse_ref, kv, keys):
    core = lax.axis_index("dp") % 2
    chunk = q_ref.shape[3]
    half = chunk // 2
    order_kv(core, own_ref, other_ref, kv)
    for c in range(4):
        for g in range(KV_HEADS):
            keys[c, g] = kv[c, g].T

    def outer(step, carry):
        g = step // 2
        s = step % 2
        mine = jnp.where(s == 0, core, 3 - core)
        lows = low_ref[s]
        qs = [q_ref[s, GROUP * g + j] for j in range(GROUP)]

        def scores(c, k0, n, q0, causal):
            key_rows = keys[c, g, k0 : k0 + n, :]
            seen = visible(c, c * chunk + k0, n, lows, q0, mine * chunk, causal)
            raw = [dot(key_rows, q[:, q0:]) for q in qs]
            return [jnp.where(seen, r, NEG) for r in raw]

        def update(c, k0, n, masked, state):
            vals = kv[c, KV_HEADS + g, :, k0 : k0 + n]
            tops = [jnp.max(m, axis=0, keepdims=True) for m in masked]
            if state is not None:
                tops = [jnp.maximum(old[0], top) for old, top in zip(state, tops)]
            probs = [jnp.exp(m - top) for m, top in zip(masked, tops)]
            lows_ = [p.astype(bf16) for p in probs]
            sums = [jnp.sum(p, axis=0, keepdims=True) for p in probs]
            mixes = [dot(vals, p) for p in lows_]
            if state is None:
                return tuple(zip(tops, sums, mixes))
            new = []
            for old, top, total, mix in zip(state, tops, sums, mixes):
                shrink = jnp.exp(old[0] - top)
                new.append((top, old[1] * shrink + total, old[2] * shrink + mix))
            return tuple(new)

        early = scores(mine, 0, half, 0, True)
        late = scores(mine, half, half, half, True)
        first = update(mine, 0, half, early, None)
        second = update(
            mine, half, half, late, [tuple(part[:, half:] for part in item) for item in first]
        )
        state = tuple(
            tuple(jnp.concatenate([a[:, :half], b], axis=1) for a, b in zip(one, two))
            for one, two in zip(first, second)
        )
        state = lax.fori_loop(
            0,
            mine,
            lambda c, now: update(c, 0, chunk, scores(c, 0, chunk, 0, False), now),
            state,
        )
        for j in range(GROUP):
            top, total, mix = state[j]
            o_ref[s, GROUP * g + j] = (mix / total).astype(bf16)
            lse_ref[s, GROUP * g + j] = top + jnp.log(total)
        return carry

    lax.fori_loop(0, 2 * KV_HEADS, outer, 0)


def attend(q, own, other, lows):
    chunk = q.shape[3]
    return pl.pallas_call(
        forward_kernel,
        out_shape=[
            jax.ShapeDtypeStruct(q.shape, bf16),
            jax.ShapeDtypeStruct((2, HEADS, 1, chunk), f32),
        ],
        in_specs=[VMEM] * 4,
        out_specs=[VMEM] * 2,
        scratch_shapes=[
            pltpu.VMEM((4, 2 * KV_HEADS, HEAD_DIM, chunk), bf16),
            pltpu.VMEM((4, KV_HEADS, chunk, HEAD_DIM), bf16),
        ],
        compiler_params=pltpu.CompilerParams(vmem_limit_bytes=56 << 20),
    )(q, own, other, lows)


def backward_kernel(
    q_ref, own_ref, other_ref, low_ref, o_ref, lse_ref, do_ref, dq_ref, mine_ref, theirs_ref,
    kv, keys, values, dkv, dq_now,
):
    core = lax.axis_index("dp") % 2
    chunk = q_ref.shape[3]
    half = chunk // 2
    order_kv(core, own_ref, other_ref, kv)
    for c in range(4):
        for g in range(KV_HEADS):
            keys[c, g] = kv[c, g].T
            values[c, g] = kv[c, KV_HEADS + g].T
        for g in range(2 * KV_HEADS):
            dkv[c, g] = jnp.zeros((HEAD_DIM, chunk), f32)

    def outer(step, carry):
        g = step // 2
        s = step % 2
        mine = jnp.where(s == 0, core, 3 - core)
        lows = low_ref[s]
        qs = [q_ref[s, GROUP * g + j] for j in range(GROUP)]
        dos = [do_ref[s, GROUP * g + j] for j in range(GROUP)]
        lses = [lse_ref[s, GROUP * g + j] for j in range(GROUP)]
        deltas = [
            jnp.sum(
                dos[j].astype(f32) * o_ref[s, GROUP * g + j].astype(f32), axis=0, keepdims=True
            )
            for j in range(GROUP)
        ]

        def block(c, k0, n, q0, causal):
            key_rows = keys[c, g, k0 : k0 + n, :]
            value_rows = values[c, g, k0 : k0 + n, :]
            key_cols = kv[c, g, :, k0 : k0 + n]
            seen = visible(c, c * chunk + k0, n, lows, q0, mine * chunk, causal)
            raw = [dot(key_rows, q[:, q0:]) for q in qs]
            dps = [dot(value_rows, d[:, q0:]) for d in dos]
            probs = [
                jnp.exp(jnp.where(seen, r, NEG) - lse[:, q0:]) for r, lse in zip(raw, lses)
            ]
            lows_ = [p.astype(bf16) for p in probs]
            dss = [
                (p * (dp - delta[:, q0:])).astype(bf16)
                for p, dp, delta in zip(probs, dps, deltas)
            ]
            dkv[c, KV_HEADS + g, :, k0 : k0 + n] += dot(
                jnp.concatenate([d[:, q0:] for d in dos], axis=1),
                jnp.concatenate(lows_, axis=1),
                NT,
            )
            dkv[c, g, :, k0 : k0 + n] += dot(
                jnp.concatenate([q[:, q0:] for q in qs], axis=1),
                jnp.concatenate(dss, axis=1),
                NT,
            )
            return [dot(key_cols, ds) for ds in dss]

        early = block(mine, 0, half, 0, True)
        late = block(mine, half, half, half, True)
        for j in range(GROUP):
            dq_now[j] = jnp.concatenate(
                [early[j][:, :half], early[j][:, half:] + late[j]], axis=1
            )

        def inner(c, carry_in):
            more = block(c, 0, chunk, 0, False)
            for j in range(GROUP):
                dq_now[j] += more[j]
            return carry_in

        lax.fori_loop(0, mine, inner, 0)
        for j in range(GROUP):
            dq_ref[s, GROUP * g + j] = 0.125 * dq_now[j]
        return carry

    lax.fori_loop(0, 2 * KV_HEADS, outer, 0)
    for core_is in range(2):

        @pl.when(core == core_is)
        def _():
            mine_ref[0] = dkv[core_is]
            mine_ref[1] = dkv[3 - core_is]
            theirs_ref[0] = dkv[1 - core_is].astype(bf16)
            theirs_ref[1] = dkv[2 + core_is].astype(bf16)


def attend_back(q, own, other, lows, o, lse, do):
    chunk = q.shape[3]
    return pl.pallas_call(
        backward_kernel,
        out_shape=[
            jax.ShapeDtypeStruct(q.shape, f32),
            jax.ShapeDtypeStruct(own.shape, f32),
            jax.ShapeDtypeStruct(own.shape, bf16),
        ],
        in_specs=[VMEM] * 7,
        out_specs=[VMEM] * 3,
        scratch_shapes=[
            pltpu.VMEM((4, 2 * KV_HEADS, HEAD_DIM, chunk), bf16),
            pltpu.VMEM((4, KV_HEADS, chunk, HEAD_DIM), bf16),
            pltpu.VMEM((4, KV_HEADS, chunk, HEAD_DIM), bf16),
            pltpu.VMEM((4, 2 * KV_HEADS, HEAD_DIM, chunk), f32),
            pltpu.VMEM((GROUP, HEAD_DIM, chunk), f32),
        ],
        compiler_params=pltpu.CompilerParams(vmem_limit_bytes=58 << 20),
    )(q, own, other, lows, o, lse, do)


def feed_kernel(
    x_ref, o_ref, dy_ref, wide_ref, down_ref, out_ref, dm_ref, do_ref, gwide_ref, gdown_ref,
    act_s, dgu_s, a_s, dm_s, gain_s,
):
    rows_all, model = x_ref.shape
    hidden = down_ref.shape[0]
    inner = o_ref.shape[1]
    block = 256
    per = o_ref.shape[2] // block
    comb0 = 2 * hidden
    tile = (comb0 + model) // 128 * 128
    lane = comb0 + model - tile
    gain = column_row(wide_ref[:, tile : tile + 128], lane, model)
    gain_s[...] = jnp.zeros_like(gain_s)
    pieces = 3
    size = hidden // pieces

    def one(t, carry):
        rows = pl.ds(pl.multiple_of(t * block, block), block)
        cols = pl.ds(pl.multiple_of((t % per) * block, block), block)
        comb = wide_ref[:, comb0 : comb0 + model]
        m = x_ref[rows, :].astype(f32) + dot(o_ref[t // per, :, cols].T, comb)
        rho = lax.rsqrt(jnp.mean(m * m, axis=1, keepdims=True) + norm_eps)
        n = m * rho
        a = (n * gain).astype(bf16)
        a_s[rows, :] = a
        dy = dy_ref[rows, :]
        total = m
        da = None
        for f in range(pieces):
            low, high = f * size, (f + 1) * size
            w_g = wide_ref[:, low:high]
            w_u = wide_ref[:, hidden + low : hidden + high]
            w_d = down_ref[low:high, :]
            g = dot(a, w_g)
            u = dot(a, w_u)
            dact = dot(dy, w_d, NT)
            sig = 0.5 * jnp.tanh(0.5 * g) + 0.5
            silu = g * sig
            act = (silu * u).astype(bf16)
            du = (dact * silu).astype(bf16)
            dg = (dact * u * (sig + silu * (1.0 - sig))).astype(bf16)
            act_s[rows, low:high] = act
            dgu_s[rows, low:high] = dg
            dgu_s[rows, hidden + low : hidden + high] = du
            total = total + dot(act, w_d)
            part = dot(dg, w_g, NT) + dot(du, w_u, NT)
            da = part if da is None else da + part
        out_ref[rows, :] = total.astype(bf16)
        gain_s[...] += jnp.sum(da * n, axis=0, keepdims=True)
        dn = da * gain
        dm = dy.astype(f32) + rho * (dn - n * jnp.mean(dn * n, axis=1, keepdims=True))
        dm_ref[rows, :] = dm
        dm_low = dm.astype(bf16)
        dm_s[rows, :] = dm_low
        do_ref[t // per, :, cols] = dot(comb, dm_low, NT).astype(bf16)
        return carry

    lax.fori_loop(0, rows_all // block, one, 0)
    rows_d = 384

    def down_grad(i, carry):
        rows = pl.ds(pl.multiple_of(i * rows_d, 128), rows_d)
        gdown_ref[rows, :] = dot(act_s[:, rows].T, dy_ref[...]).astype(bf16)
        return carry

    lax.fori_loop(0, hidden // rows_d, down_grad, 0)
    a_t = a_s[...].T
    cols_w = 512

    def wide_grad(i, carry):
        cols = pl.ds(pl.multiple_of(i * cols_w, 128), cols_w)
        gwide_ref[:, cols] = dot(a_t, dgu_s[:, cols]).astype(bf16)
        return carry

    lax.fori_loop(0, 2 * hidden // cols_w, wide_grad, 0)
    chunk = o_ref.shape[2]
    comb_grad = dot(o_ref[0], dm_s[:chunk, :]) + dot(o_ref[1], dm_s[chunk:, :])
    gain_col = jnp.broadcast_to(gain_s[...], (128, model)).T
    end = gwide_ref.shape[1]
    gwide_ref[:, comb0:tile] = comb_grad[:, : tile - comb0].astype(bf16)
    gwide_ref[:, tile:end] = jnp.concatenate(
        [
            comb_grad[:, tile - comb0 :],
            gain_col[:, : 128 - lane],
            jnp.zeros((inner, end - tile - 128), f32),
        ],
        axis=1,
    ).astype(bf16)


def feed(x, o, dy, wide, down):
    rows, model = x.shape
    hidden = down.shape[0]
    return pl.pallas_call(
        feed_kernel,
        out_shape=[
            jax.ShapeDtypeStruct((rows, model), bf16),
            jax.ShapeDtypeStruct((rows, model), f32),
            jax.ShapeDtypeStruct(o.shape, bf16),
            jax.ShapeDtypeStruct(wide.shape, bf16),
            jax.ShapeDtypeStruct(down.shape, bf16),
        ],
        in_specs=[VMEM] * 5,
        out_specs=[VMEM] * 5,
        scratch_shapes=[
            pltpu.VMEM((rows, hidden), bf16),
            pltpu.VMEM((rows, 2 * hidden), bf16),
            pltpu.VMEM((rows, model), bf16),
            pltpu.VMEM((rows, model), bf16),
            pltpu.VMEM((1, model), f32),
        ],
        compiler_params=pltpu.CompilerParams(vmem_limit_bytes=60 << 20),
    )(x, o, dy, wide, down)


def qkv_back_kernel(
    inner, x_ref, dm_ref, dq_ref, own_ref, other_ref, cos_ref, sin_ref, w_ref, dx_ref, gw_ref
):
    model = x_ref.shape[2]
    width = inner + 2 * KV_HEADS * HEAD_DIM
    tile = width // 128 * 128
    lane = width - tile
    gain = column_row(w_ref[:, tile : tile + 128], lane, model)
    w = w_ref[:, :width]
    grad = None
    gain_grad = None
    for s in range(2):
        cos = cos_ref[s]
        sin = sin_ref[s]

        def back(d):
            d1 = d[:HALF]
            d2 = d[HALF:]
            return jnp.concatenate([d1 * cos + d2 * sin, d2 * cos - d1 * sin], axis=0)

        parts = [back(dq_ref[s, head]) for head in range(HEADS)]
        full = [own_ref[s, head] + other_ref[s, head].astype(f32) for head in range(2 * KV_HEADS)]
        parts += [back(full[head]) for head in range(KV_HEADS)]
        parts += full[KV_HEADS:]
        dz_t = jnp.concatenate([part.astype(bf16) for part in parts], axis=0)
        x = x_ref[s].astype(f32)
        rho = lax.rsqrt(jnp.mean(x * x, axis=1, keepdims=True) + norm_eps)
        n = x * rho
        a = (n * gain).astype(bf16)
        da = dot(dz_t.T, w, NT)
        part = dot(a.T, dz_t, NT)
        grad = part if grad is None else grad + part
        part = jnp.sum(da * n, axis=0, keepdims=True)
        gain_grad = part if gain_grad is None else gain_grad + part
        dn = da * gain
        dx = dm_ref[s] + rho * (dn - n * jnp.mean(dn * n, axis=1, keepdims=True))
        dx_ref[s] = dx.astype(bf16)
    gain_col = jnp.broadcast_to(gain_grad, (128, model)).T
    gw_ref[:, :tile] = grad[:, :tile].astype(bf16)
    gw_ref[:, tile:] = jnp.concatenate(
        [grad[:, tile:], gain_col[:, : gw_ref.shape[1] - width]], axis=1
    ).astype(bf16)


def project_back(x, dm, dq, own, other, cos, sin, w):
    return pl.pallas_call(
        functools.partial(qkv_back_kernel, HEADS * HEAD_DIM),
        out_shape=[jax.ShapeDtypeStruct(x.shape, bf16), jax.ShapeDtypeStruct(w.shape, bf16)],
        in_specs=[VMEM] * 8,
        out_specs=[VMEM] * 2,
        compiler_params=pltpu.CompilerParams(vmem_limit_bytes=58 << 20),
    )(x, dm, dq, own, other, cos, sin, w)


def routes(dp_size, seq_size):
    first, second = [], []
    taker = {0: 0, 3: 0, 1: 1, 2: 1}
    for dp in range(dp_size):
        core = dp % 2
        for j in range(4):
            k = 0 if j < 2 else 1
            source = dp * seq_size + j
            target = dp - core + taker[j]
            first.append((source, target * seq_size + 2 * core + k))
            second.append((source, target * seq_size + 2 * core + 1 - k))
    return first, second


def swap(pair, flip, perms):
    one = jnp.where(flip, pair[1], pair[0])
    two = jnp.where(flip, pair[0], pair[1])
    return (
        lax.ppermute(one, ("dp", "seq"), perms[0]),
        lax.ppermute(two, ("dp", "seq"), perms[1]),
    )


def unswap(one, two, flip):
    return jnp.stack([jnp.where(flip, two, one), jnp.where(flip, one, two)])


def adam_step(master, grad_total, mean_old, square_old, decays):
    mean_new = beta_one * mean_old + (1.0 - beta_one) * grad_total
    square_new = beta_two * square_old + (1.0 - beta_two) * grad_total * grad_total
    mean_hat = mean_new / (1.0 - beta_one**STEP)
    square_hat = square_new / (1.0 - beta_two**STEP)
    change = mean_hat / (jnp.sqrt(square_hat) + adam_eps)
    if decays:
        change = change + decay_rate * master
    return (master - learn_rate * change, mean_new, square_new)


def pad_cols(pieces, width):
    rows = pieces[0].shape[0]
    used = sum(piece.shape[1] for piece in pieces)
    return jnp.concatenate(
        [piece.astype(bf16) for piece in pieces] + [jnp.zeros((rows, width - used), bf16)], axis=1
    )


def on_device(
    tokens, positions, cotangent,
    balance, projector, combiner, leveler, expander, reducer,
    mean_balance, mean_projector, mean_combiner, mean_leveler, mean_expander, mean_reducer,
    square_balance, square_projector, square_combiner, square_leveler, square_expander,
    square_reducer,
):
    dp_size = lax.axis_size("dp")
    seq_size = lax.axis_size("seq")
    z = lax.axis_index("seq")
    core = lax.axis_index("dp") % 2
    _, chunk, model = tokens.shape
    width = projector.shape[1]
    hidden2 = expander.shape[1]
    inner = combiner.shape[1]
    perms = routes(dp_size, seq_size)
    backs = [[(b, a) for a, b in perm] for perm in perms]
    late = z >= 2
    odd = z % 2 == 1

    x1 = unswap(*swap(tokens, late, perms), odd)
    pos1 = unswap(*swap(positions, late, perms), odd)

    wide_part = pad_cols([expander, combiner, leveler[:, None]], 4096)
    proj_part = pad_cols([projector, balance[:, None]], 1024)
    wide, down, proj = gather_weights(
        [wide_part, reducer.astype(bf16), proj_part], [False, True, False], 0
    )

    inverse = jnp.power(rope_base, -jnp.arange(HALF, dtype=f32) * (2.0 / HEAD_DIM))
    phases = pos1.astype(f32)[:, None, :] * inverse[None, :, None]
    cos = jnp.cos(phases)
    sin = jnp.sin(phases)
    starts = jnp.stack([core * chunk, (3 - core) * chunk])
    index = starts[:, None] + jnp.arange(chunk, dtype=jnp.int32)[None, :]
    lows = (index - pos1)[:, None, :]

    q, own = project(x1, proj, cos, sin)
    dy_in, own = lax.optimization_barrier((cotangent, own))
    siblings = [
        (dp * seq_size + s, (dp + 1 - 2 * (dp % 2)) * seq_size + s)
        for dp in range(dp_size)
        for s in range(seq_size)
    ]
    other = lax.ppermute(own, ("dp", "seq"), siblings)
    dy1 = unswap(*swap(dy_in, late, perms), odd)
    o, lse = attend(q, own, other, lows)
    out1, dm, do, gwide, gdown = feed(
        x1.reshape(2 * chunk, model),
        o.reshape(2, inner, chunk),
        dy1.reshape(2 * chunk, model),
        wide,
        down,
    )
    out1 = out1.reshape(2, chunk, model)
    layer_out = unswap(*swap(out1, odd, backs), late)
    dq, own_grad, send_grad = attend_back(q, own, other, lows, o, lse, do.reshape(o.shape))
    other_grad = lax.ppermute(send_grad, ("dp", "seq"), siblings)
    dx1, gproj = project_back(
        x1, dm.reshape(2, chunk, model), dq, own_grad, other_grad, cos, sin, proj
    )
    tokens_grad = unswap(*swap(dx1, odd, backs), late)
    swide, sdown = scatter_grads([gwide, gdown], [False, True], 1)
    (sproj,) = scatter_grads([gproj], [False], 2)
    if dp_size > 8:
        groups = [[g * 8 + k for g in range(dp_size // 8)] for k in range(8)]
        swide, sdown, sproj = (
            lax.psum(part, "dp", axis_index_groups=groups) for part in (swide, sdown, sproj)
        )
    swide, sdown, sproj = (part.astype(f32) for part in (swide, sdown, sproj))
    totals = (
        sproj[:, width],
        sproj[:, :width],
        swide[:, hidden2 : hidden2 + inner],
        swide[:, hidden2 + inner],
        swide[:, :hidden2],
        sdown,
    )
    masters = (balance, projector, combiner, leveler, expander, reducer)
    means = (mean_balance, mean_projector, mean_combiner, mean_leveler, mean_expander, mean_reducer)
    squares = (
        square_balance, square_projector, square_combiner, square_leveler, square_expander,
        square_reducer,
    )
    decay_flags = (False, True, True, False, True, True)
    results = [
        adam_step(master, total, mean, square, decays)
        for master, total, mean, square, decays in zip(
            masters, totals, means, squares, decay_flags
        )
    ]
    return (
        (layer_out, tokens_grad)
        + totals
        + tuple(result[0] for result in results)
        + tuple(result[1] for result in results)
        + tuple(result[2] for result in results)
    )


def solution(mesh):
    vector, matrix = P("seq"), P("seq", None)
    weights = (vector, matrix, matrix, vector, matrix, matrix)
    rows = P("dp", "seq", None)
    return jax.shard_map(
        on_device,
        mesh=mesh,
        in_specs=(rows, P("dp", "seq"), rows) + weights * 3,
        out_specs=(rows, rows) + weights * 4,
        check_vma=False,
    )
```

time: 972 us -> 402 us (0.41)
  local copies, waits for them, and re-layouts: 323 us -> 34.2 us
  Pallas kernels: 0 us -> 274 us
  matrix products: 271 us -> 0 us
  waiting for transfers between devices: 158 us -> 2.78 us
  other arithmetic: 131 us -> 39 us
  blocking collectives: 65 us -> 0 us
  starting transfers between devices: 0.75 us -> 48 us
  between operations: 16.7 us -> 1.13 us
    unnamed x146 -> x55, local copies, waits for them, and re-layouts: 303 us -> 15.1 us
    pallas_call x0 -> x8, Pallas kernels: none -> 274 us  [the longest x2 95.9 us: scatter_grads(): pl.pallas_call(functools.partial(scatter_kernel, count, blocks), out_shap...]
    dot_general x24 -> x0, matrix products: 271 us -> none  [the longest x2 58.5 us: on_device(): jnp.einsum('qgjd,kgd->gjqk', heads_grad[number], value_heads, preferred_e...]
    reduce_scatter x4 -> x0, waiting for transfers between devices: 71.5 us -> none  [the longest x1 67.4 us: on_device(): lax.psum_scatter(grads[4].astype(jnp.bfloat16), 'seq', scatter_dimension=...]
    convert_element_type x10 -> x9, other arithmetic: 72.2 us -> 7.3 us  [the longest x2 3.98 us: on_device(): swide, sdown, sproj = (part.astype(f32) for part in (swide, sdown, sproj))]
    all_gather x5 -> x0, waiting for transfers between devices: 48.5 us -> none  [the longest x1 30.4 us: on_device(): lax.all_gather(reducer.astype(jnp.bfloat16), 'seq', axis=0, tiled=True)]
    ppermute x0 -> x12, starting transfers between devices: none -> 48 us  [the longest x5 24.5 us: swap(): lax.ppermute(one, ('dp', 'seq'), perms[0])]
    psum x1 -> x0, waiting for transfers between devices: 36.8 us -> none  [on_device(): lax.psum(slices[1].astype(jnp.bfloat16), 'dp').astype(jnp.float32)]
  transfers between devices with their start and end apart: 12 -> 12, of which waited for: 8 -> 1; matrix products, arithmetic and copies ran while one was open for 55% -> 16% of each run, Pallas kernels for 0% -> 43%
where the time goes in v1:
time: 402 us; the launch traced here: 400 us
  Pallas kernels  274 us (68%)
  starting transfers between devices  48 us (12%)
  other arithmetic  39 us (10%)
  local copies, waits for them, and re-layouts  34.2 us (9%)
    pallas_call x2, Pallas kernels, scatter_grads(): pl.pallas_call(functools.partial(scatter_kernel, count, blocks), out_shap...  95.9 us
    pallas_call x1, Pallas kernels, gather_weights(): pl.pallas_call(functools.partial(gather_kernel, count, blocks), out_shape...  67 us
    pallas_call x1, Pallas kernels, feed(): pl.pallas_call(feed_kernel, out_shape=[jax.ShapeDtypeStruct((rows, model)...  37.7 us
    pallas_call x1, Pallas kernels, attend_back(): pl.pallas_call(backward_kernel, out_shape=[jax.ShapeDtypeStruct(q.shape,...  37 us
    ppermute x5, starting transfers between devices, swap(): lax.ppermute(one, ('dp', 'seq'), perms[0])  24.5 us
    pallas_call x1, Pallas kernels, attend(): pl.pallas_call(forward_kernel, out_shape=[jax.ShapeDtypeStruct(q.shape, b...  23.4 us
    ppermute x5, starting transfers between devices, swap(): lax.ppermute(two, ('dp', 'seq'), perms[1])  16.5 us
    unnamed x55, local copies, waits for them, and re-layouts  15.1 us
  transfers between devices with their start and end apart: 12, of which 1 were waited for; matrix products, arithmetic and copies ran while one was open for 16% of the time, Pallas kernels for 43%

profile of v1, /device:TPU:0, one launch (start us, length us, event | category | flops | bytes accessed | tf_op | source)
XLA Modules:
  0.0 399.6 jit_solution(17144006840575443095)
XLA Ops:
  0.7 2.5 select_bitcast_fusion.13
  3.2 4.9 %collective-permute-start = (bf16[512,576]{0,1:T(8,128)(2,1)}, bf16[512,576]{0,1:T(8,128)(2,1)}, u32[]{:S(2)}, u32[]{:S(2)}) collective-permute-start(bf16[512,576]{0,1:T(8,128)(2,1)} %get-tuple-element.207), channel_id=1, source_target_pairs={{0,1},{1,5},{2,4},{3,0},{4,3},{5,7},{6,6},{7,2},{8,9},{9,13},{10,1... | collective-permute-start | bytes 1769480 | tf_op jit(solution)/shard_map/ppermute | solution.py:763
  8.1 6.0 %collective-permute-start.1 = (bf16[512,576]{0,1:T(8,128)(2,1)}, bf16[512,576]{0,1:T(8,128)(2,1)}, u32[]{:S(2)}, u32[]{:S(2)}) collective-permute-start(bf16[512,576]{0,1:T(8,128)(2,1)} %get-tuple-element.208), channel_id=1, source_target_pairs={{0,0},{1,4},{2,5},{3,1},{4,2},{5,6},{6,7},{7,3},{8,8},{9,12},{10,1... | collective-permute-start | bytes 1769480 | tf_op jit(solution)/shard_map/ppermute | solution.py:762
  14.1 1.9 collective-permute-start.2
  18.4 1.7 convert_element_type.41
  22.3 2.0 copy.108.refs_1_
  24.3 2.8 concatenate.17.refs_0_
  27.1 67.0 %shard_map.404 = (bf16[576,4096]{1,0:T(8,128)(2,1)}, bf16[1536,576]{1,0:T(8,128)(2,1)}, bf16[576,1024]{1,0:T(8,128)(2,1)}) custom-call(bf16[144,4096]{1,0:T(8,128)(2,1)} %concatenate.17.refs_0_, bf16[384,576]{1,0:T(8,128)(2,1)} %copy.108.refs_1_, bf16[144,1024]{1,0:T(8,128)(2,1)} %maximum_maximum_fusion.refs_2_), custom_call_target="tpu_custom_call" | custom-call | tf_op jit(solution)/shard_map/pallas_call | solution.py:160
  94.2 1.2 multiply_sine_fusion
  95.4 1.4 copy.102
  96.8 1.4 copy.103
  98.3 1.3 pad_maximum_fusion.x_ref
  99.6 5.0 %shard_map.405 = (bf16[2,9,64,512]{3,2,1,0:T(8,128)(2,1)}, bf16[2,6,64,512]{3,2,1,0:T(8,128)(2,1)}) custom-call(bf16[2,512,576]{2,1,0:T(8,128)(2,1)} %pad_maximum_fusion.x_ref, bf16[576,1024]{1,0:T(8,128)(2,1)} %get-tuple-element.47.w_ref, f32[2,32,512]{2,1,0:T(8,128)} %get-tuple-element.210.cos_ref, f32[2,32,512]{2,1,0:T(8,128)} %get-tuple-element.209.sin_ref), custom_call_target="tpu_custom_call" | custom-call | tf_op jit(solution)/shard_map/pallas_call | solution.py:350
  105.7 2.5 collective-permute-start.5
  108.1 6.0 %collective-permute-start.6 = (bf16[512,576]{0,1:T(8,128)(2,1)}, bf16[512,576]{0,1:T(8,128)(2,1)}, u32[]{:S(2)}, u32[]{:S(2)}) collective-permute-start(bf16[512,576]{0,1:T(8,128)(2,1)} %get-tuple-element.206), channel_id=1, source_target_pairs={{0,0},{1,4},{2,5},{3,1},{4,2},{5,6},{6,7},{7,3},{8,8},{9,12},{10,1... | collective-permute-start | bytes 1769480 | tf_op jit(solution)/shard_map/ppermute | solution.py:762
  114.1 1.5 copy.120
  115.6 2.4 copy.117
  118.1 2.5 copy.118
  121.3 2.8 collective-permute-done.5
  124.1 2.1 copy.109
  126.2 2.1 copy.110
  128.4 1.4 select_bitcast_fusion.3
  129.8 1.3 pad_maximum_fusion.1
  131.0 23.4 %shard_map.406 = (bf16[2,9,64,512]{3,2,1,0:T(8,128)(2,1)}, f32[2,9,1,512]{3,2,1,0:T(1,128)}) custom-call(bf16[2,9,64,512]{3,2,1,0:T(8,128)(2,1)} %get-tuple-element.48.q_ref, bf16[2,6,64,512]{3,2,1,0:T(8,128)(2,1)} %get-tuple-element.50.own_ref, bf16[2,6,64,512]{3,2,1,0:T(8,128)(2,1)} %collective-permute-done.4.other_ref, s32[2,1,512]{2,1,0:T(1,128)} %add_subtract_fusion.low_ref), custom_call_target="tpu_custom_call" | custom-call | tf_op jit(solution)/shard_map/pallas_call | solution.py:450
  154.4 37.7 %shard_map.407 = (bf16[1024,576]{1,0:T(8,128)(2,1)}, f32[1024,576]{1,0:T(8,128)}, bf16[2,576,512]{2,1,0:T(8,128)(2,1)}, bf16[576,4096]{1,0:T(8,128)(2,1)}, bf16[1536,576]{1,0:T(8,128)(2,1)}) custom-call(bf16[1024,576]{1,0:T(8,128)(2,1)} %bitcast.44, bf16[2,576,512]{2,1,0:T(8,128)(2,1)} %bitcast.46, bf16[1024,576]{1,0:T(8,128)(2,1)} %bitcast.45, ...), custom_call_target="tpu_custom_call" | custom-call | tf_op jit(solution)/shard_map/pallas_call | solution.py:668
  192.1 37.0 %shard_map.408 = (f32[2,9,64,512]{3,2,1,0:T(8,128)}, f32[2,6,64,512]{3,2,1,0:T(8,128)}, bf16[2,6,64,512]{3,2,1,0:T(8,128)(2,1)}) custom-call(bf16[2,9,64,512]{3,2,1,0:T(8,128)(2,1)} %get-tuple-element.48.q_ref, bf16[2,6,64,512]{3,2,1,0:T(8,128)(2,1)} %get-tuple-element.50.own_ref, bf16[2,6,64,512]{3,2,1,0:T(8,128)(2,1)} %collective-permute-done.4.other_ref, ...), custom_call_target="tpu_custom_call" | custom-call | tf_op jit(solution)/shard_map/pallas_call | solution.py:554
  229.1 7.0 %collective-permute-start.9 = (bf16[2,6,64,512]{3,2,1,0:T(8,128)(2,1)}, bf16[2,6,64,512]{3,2,1,0:T(8,128)(2,1)}, u32[]{:S(2)}, u32[]{:S(2)}) collective-permute-start(bf16[2,6,64,512]{3,2,1,0:T(8,128)(2,1)} %get-tuple-element.61), channel_id=1, source_target_pairs={{0,4},{1,5},{2,6},{3,7},{4,0},{5,1},{6,2},{7,3},{8,12},{9,13},{10,... | collective-permute-start | bytes 2359304 | tf_op jit(solution)/shard_map/ppermute | solution.py:847
  237.1 2.1 copy.114
  239.2 5.9 %collective-permute-start.8 = (bf16[512,576]{0,1:T(8,128)(2,1)}, bf16[512,576]{0,1:T(8,128)(2,1)}, u32[]{:S(2)}, u32[]{:S(2)}) collective-permute-start(bf16[512,576]{0,1:T(8,128)(2,1)} %copy.114), channel_id=1, source_target_pairs={{0,0},{4,1},{5,2},{1,3},{2,4},{6,5},{7,6},{3,7},{8,8},{12,9},{13,1... | collective-permute-start | bytes 1769480 | tf_op jit(solution)/shard_map/ppermute | solution.py:762
  246.2 1.9 collective-permute-start.7
  248.1 65.3 %shard_map.411 = (bf16[144,4096]{1,0:T(8,128)(2,1)}, bf16[384,576]{1,0:T(8,128)(2,1)}) custom-call(bf16[4,144,4096]{2,1,0:T(8,128)(2,1)} %bitcast.47, bf16[4,384,576]{2,1,0:T(8,128)(2,1)} %bitcast.49), custom_call_target="tpu_custom_call" | custom-call | tf_op jit(solution)/shard_map/pallas_call | solution.py:304
  313.4 3.0 convert_element_type.50
  317.5 3.6 multiply_subtract_fusion.1
  321.1 2.4 copy.122
  323.5 2.5 copy.123
  326.1 2.4 copy.124
  328.5 2.4 multiply_subtract_fusion.3
  330.9 4.9 %multiply_subtract_fusion = (f32[144,3072]{1,0:T(8,128)}, f32[144,3072]{1,0:T(8,128)}, f32[144,3072]{1,0:T(8,128)}, f32[144,3072]{1,0:T(8,128)}) fusion(f32[144,3072]{1,0:T(8,128)S(1)} %copy-done.1, f32[144,3072]{1,0:T(8,128)S(1)} %copy-done.7, f32[144,3072]{1,0:T(8,128)} %param.40, bf16[144,4096]{1,0:T(8,128)(2,1)S(1)} %copy-done), kind=kLoop, calls=%fused_computation.2 | loop fusion | flops 6635520 | bytes 14155776 | tf_op jit(solution)/shard_map/sub | solution.py:779
  335.9 8.3 %shard_map.409 = (bf16[2,512,576]{2,1,0:T(8,128)(2,1)}, bf16[576,1024]{1,0:T(8,128)(2,1)}) custom-call(bf16[2,512,576]{2,1,0:T(8,128)(2,1)} %pad_maximum_fusion.x_ref, f32[2,512,576]{2,1,0:T(8,128)} %bitcast.48, f32[2,9,64,512]{3,2,1,0:T(8,128)} %get-tuple-element.59.dq_ref, f32[2,6,64,512]{3,2,1,0:T(8,128)} %get-tuple-element.60.own_ref, ...), custom_call_target="tpu_custom_call" | custom-call | tf_op jit(solution)/shard_map/pallas_call | solution.py:735
  344.2 1.4 select_bitcast_fusion.1
  346.7 5.3 %collective-permute-start.10 = (bf16[512,576]{0,1:T(8,128)(2,1)}, bf16[512,576]{0,1:T(8,128)(2,1)S(1)}, u32[]{:S(2)}, u32[]{:S(2)}) collective-permute-start(bf16[512,576]{0,1:T(8,128)(2,1)} %copy.115), channel_id=1, source_target_pairs={{1,0},{5,1},{4,2},{0,3},{3,4},{7,5},{6,6},{2,7},{9,8},{13,9},{12,1... | collective-permute-start | bytes 1769480 | tf_op jit(solution)/shard_map/ppermute | solution.py:763
  353.1 6.0 %collective-permute-start.11 = (bf16[512,576]{0,1:T(8,128)(2,1)}, bf16[512,576]{0,1:T(8,128)(2,1)}, u32[]{:S(2)}, u32[]{:S(2)}) collective-permute-start(bf16[512,576]{0,1:T(8,128)(2,1)} %copy.116), channel_id=1, source_target_pairs={{0,0},{4,1},{5,2},{1,3},{2,4},{6,5},{7,6},{3,7},{8,8},{12,9},{13,1... | collective-permute-start | bytes 1769480 | tf_op jit(solution)/shard_map/ppermute | solution.py:762
  359.1 30.7 %shard_map.410 = bf16[144,1024]{1,0:T(8,128)(2,1)} custom-call(bf16[4,144,1024]{2,1,0:T(8,128)(2,1)} %bitcast.51), custom_call_target="tpu_custom_call" | custom-call | tf_op jit(solution)/shard_map/pallas_call | solution.py:304
  390.8 1.1 slice_reduce_fusion
  393.2 2.5 multiply_subtract_fusion.2
  395.7 1.6 select_bitcast_fusion.7
  397.3 1.1 pad_maximum_fusion.2
  398.4 1.1 pad_maximum_fusion.3
  (88 shorter events, 14.1 us)
Async XLA Ops:
  0.7 13.4 %copy-start.15 = (s32[2,512]{1,0:T(2,128)S(1)}, s32[2,512]{1,0:T(2,128)}, u32[]{:S(2)}) copy-start(s32[2,512]{1,0:T(2,128)} %param.22) | copy-start | bytes 12292
  0.7 16.0 %copy-start.16 = (f32[144]{0:T(256)S(1)}, f32[144]{0:T(256)}, u32[]{:S(2)}) copy-start(f32[144]{0:T(256)} %param.24) | copy-start | bytes 1732
  0.7 16.1 %copy-start.4 = (f32[144,960]{1,0:T(8,128)S(1)}, f32[144,960]{1,0:T(8,128)}, u32[]{:S(2)}) copy-start(f32[144,960]{1,0:T(8,128)} %param.25) | copy-start | bytes 1658884
  0.7 17.6 %copy-start.1 = (f32[144,3072]{1,0:T(8,128)S(1)}, f32[144,3072]{1,0:T(8,128)}, u32[]{:S(2)}) copy-start(f32[144,3072]{1,0:T(8,128)} %param.28) | copy-start | bytes 5308420
  3.2 92.2 %collective-permute-start = (bf16[512,576]{0,1:T(8,128)(2,1)}, bf16[512,576]{0,1:T(8,128)(2,1)}, u32[]{:S(2)}, u32[]{:S(2)}) collective-permute-start(bf16[512,576]{0,1:T(8,128)(2,1)} %get-tuple-element.207), channel_id=1, source_target_pairs={{0,1},{1,5},{2,4},{3,0},{4,3},{5,7},{6,6},{7,2},{8,9},{9,13},{10,1... | collective-permute-start | bytes 1769480 | tf_op jit(solution)/shard_map/ppermute | solution.py:763
  8.1 88.7 %collective-permute-start.1 = (bf16[512,576]{0,1:T(8,128)(2,1)}, bf16[512,576]{0,1:T(8,128)(2,1)}, u32[]{:S(2)}, u32[]{:S(2)}) collective-permute-start(bf16[512,576]{0,1:T(8,128)(2,1)} %get-tuple-element.208), channel_id=1, source_target_pairs={{0,0},{1,4},{2,5},{3,1},{4,2},{5,6},{6,7},{7,3},{8,8},{9,12},{10,1... | collective-permute-start | bytes 1769480 | tf_op jit(solution)/shard_map/ppermute | solution.py:762
  14.1 80.0 %collective-permute-start.2 = (s32[512]{0:T(512)S(1)}, s32[512]{0:T(512)S(1)}, u32[]{:S(2)}, u32[]{:S(2)}) collective-permute-start(s32[512]{0:T(512)S(1)} %bitcast.57), channel_id=1, source_target_pairs={{0,1},{1,5},{2,4},{3,0},{4,3},{5,7},{6,6},{7,2},{8,9},{9,13},{10,1... | collective-permute-start | bytes 6152 | tf_op jit(solution)/shard_map/ppermute | solution.py:763
  16.0 78.1 %collective-permute-start.3 = (s32[512]{0:T(512)S(1)}, s32[512]{0:T(512)S(1)}, u32[]{:S(2)}, u32[]{:S(2)}) collective-permute-start(s32[512]{0:T(512)S(1)} %bitcast.56), channel_id=1, source_target_pairs={{0,0},{1,4},{2,5},{3,1},{4,2},{5,6},{6,7},{7,3},{8,8},{9,12},{10,1... | collective-permute-start | bytes 6152 | tf_op jit(solution)/shard_map/ppermute | solution.py:762
  17.8 3.7 copy-start.2
  24.3 69.9 %copy-start.23 = (f32[32]{0:T(128)S(1)}, f32[32]{0:T(128)}, u32[]{:S(2)}) copy-start(f32[32]{0:T(128)} %multiply_power_fusion) | copy-start | bytes 388
  99.5 5.0 %copy-start.10 = (bf16[2,512,576]{1,2,0:T(8,128)(2,1)S(1)}, bf16[2,512,576]{1,2,0:T(8,128)(2,1)}, u32[]{:S(2)}) copy-start(bf16[2,512,576]{1,2,0:T(8,128)(2,1)} %param.23) | copy-start | bytes 3538948
  104.6 9.5 %copy-start.3 = (bf16[2,6,64,512]{3,2,1,0:T(8,128)(2,1)S(1)}, bf16[2,6,64,512]{3,2,1,0:T(8,128)(2,1)}, u32[]{:S(2)}) copy-start(bf16[2,6,64,512]{3,2,1,0:T(8,128)(2,1)} %get-tuple-element.50.own_ref) | copy-start | bytes 2359300
  105.7 18.4 %collective-permute-start.5 = (bf16[512,576]{0,1:T(8,128)(2,1)}, bf16[512,576]{0,1:T(8,128)(2,1)}, u32[]{:S(2)}, u32[]{:S(2)}) collective-permute-start(bf16[512,576]{0,1:T(8,128)(2,1)} %get-tuple-element.205), channel_id=1, source_target_pairs={{0,1},{1,5},{2,4},{3,0},{4,3},{5,7},{6,6},{7,2},{8,9},{9,13},{10,1... | collective-permute-start | bytes 1769480 | tf_op jit(solution)/shard_map/ppermute | solution.py:763
  108.1 18.1 %collective-permute-start.6 = (bf16[512,576]{0,1:T(8,128)(2,1)}, bf16[512,576]{0,1:T(8,128)(2,1)}, u32[]{:S(2)}, u32[]{:S(2)}) collective-permute-start(bf16[512,576]{0,1:T(8,128)(2,1)} %get-tuple-element.206), channel_id=1, source_target_pairs={{0,0},{1,4},{2,5},{3,1},{4,2},{5,6},{6,7},{7,3},{8,8},{9,12},{10,1... | collective-permute-start | bytes 1769480 | tf_op jit(solution)/shard_map/ppermute | solution.py:762
  114.1 16.9 %collective-permute-start.4 = (bf16[2,6,64,512]{3,2,1,0:T(8,128)(2,1)S(1)}, bf16[2,6,64,512]{3,2,1,0:T(8,128)(2,1)}, u32[]{:S(2)}, u32[]{:S(2)}) collective-permute-start(bf16[2,6,64,512]{3,2,1,0:T(8,128)(2,1)S(1)} %copy-done.3), channel_id=1, source_target_pairs={{0,4},{1,5},{2,6},{3,7},{4,0},{5,1},{6,2},{7,3},{8,12},{9,13},{10,... | collective-permute-start | bytes 2359304 | tf_op jit(solution)/shard_map/ppermute | solution.py:834
  192.1 44.0 %copy-start.9 = (bf16[1024,576]{1,0:T(8,128)(2,1)S(1)}, bf16[1024,576]{1,0:T(8,128)(2,1)}, u32[]{:S(2)}) copy-start(bf16[1024,576]{1,0:T(8,128)(2,1)} %get-tuple-element.55) | copy-start | bytes 3538948
  229.1 106.8 %collective-permute-start.9 = (bf16[2,6,64,512]{3,2,1,0:T(8,128)(2,1)}, bf16[2,6,64,512]{3,2,1,0:T(8,128)(2,1)}, u32[]{:S(2)}, u32[]{:S(2)}) collective-permute-start(bf16[2,6,64,512]{3,2,1,0:T(8,128)(2,1)} %get-tuple-element.61), channel_id=1, source_target_pairs={{0,4},{1,5},{2,6},{3,7},{4,0},{5,1},{6,2},{7,3},{8,12},{9,13},{10,... | collective-permute-start | bytes 2359304 | tf_op jit(solution)/shard_map/ppermute | solution.py:847
  239.2 156.5 %collective-permute-start.8 = (bf16[512,576]{0,1:T(8,128)(2,1)}, bf16[512,576]{0,1:T(8,128)(2,1)}, u32[]{:S(2)}, u32[]{:S(2)}) collective-permute-start(bf16[512,576]{0,1:T(8,128)(2,1)} %copy.114), channel_id=1, source_target_pairs={{0,0},{4,1},{5,2},{1,3},{2,4},{6,5},{7,6},{3,7},{8,8},{12,9},{13,1... | collective-permute-start | bytes 1769480 | tf_op jit(solution)/shard_map/ppermute | solution.py:762
  246.2 149.5 %collective-permute-start.7 = (bf16[512,576]{0,1:T(8,128)(2,1)}, bf16[512,576]{0,1:T(8,128)(2,1)}, u32[]{:S(2)}, u32[]{:S(2)}) collective-permute-start(bf16[512,576]{0,1:T(8,128)(2,1)} %copy.113), channel_id=1, source_target_pairs={{1,0},{5,1},{4,2},{0,3},{3,4},{7,5},{6,6},{2,7},{9,8},{13,9},{12,1... | collective-permute-start | bytes 1769480 | tf_op jit(solution)/shard_map/ppermute | solution.py:763
  313.4 3.0 copy-start.6
  323.5 5.0 %copy-start = (bf16[144,4096]{1,0:T(8,128)(2,1)S(1)}, bf16[144,4096]{1,0:T(8,128)(2,1)}, u32[]{:S(2)}) copy-start(bf16[144,4096]{1,0:T(8,128)(2,1)} %get-tuple-element.66) | copy-start | bytes 3538948
  323.5 5.0 %copy-start.8 = (f32[144,576]{1,0:T(8,128)S(1)}, f32[144,576]{1,0:T(8,128)}, u32[]{:S(2)}) copy-start(f32[144,576]{1,0:T(8,128)} %param.26) | copy-start | bytes 995332
  328.5 2.4 copy-start.7
  346.7 49.1 %collective-permute-start.10 = (bf16[512,576]{0,1:T(8,128)(2,1)}, bf16[512,576]{0,1:T(8,128)(2,1)S(1)}, u32[]{:S(2)}, u32[]{:S(2)}) collective-permute-start(bf16[512,576]{0,1:T(8,128)(2,1)} %copy.115), channel_id=1, source_target_pairs={{1,0},{5,1},{4,2},{0,3},{3,4},{7,5},{6,6},{2,7},{9,8},{13,9},{12,1... | collective-permute-start | bytes 1769480 | tf_op jit(solution)/shard_map/ppermute | solution.py:763
  351.9 40.0 %copy-start.17 = (f32[144]{0:T(256)S(1)}, f32[144]{0:T(256)}, u32[]{:S(2)}) copy-start(f32[144]{0:T(256)} %param.24) | copy-start | bytes 1732
  351.9 40.0 %copy-start.18 = (f32[144]{0:T(256)S(1)}, f32[144]{0:T(256)}, u32[]{:S(2)}) copy-start(f32[144]{0:T(256)} %param.30) | copy-start | bytes 1732
  351.9 40.0 %copy-start.19 = (f32[144]{0:T(256)S(1)}, f32[144]{0:T(256)}, u32[]{:S(2)}) copy-start(f32[144]{0:T(256)} %param.36) | copy-start | bytes 1732
  352.0 40.6 %copy-start.20 = (f32[144]{0:T(256)S(1)}, f32[144]{0:T(256)}, u32[]{:S(2)}) copy-start(f32[144]{0:T(256)} %param.27) | copy-start | bytes 1732
  352.0 40.6 %copy-start.21 = (f32[144]{0:T(256)S(1)}, f32[144]{0:T(256)}, u32[]{:S(2)}) copy-start(f32[144]{0:T(256)} %param.33) | copy-start | bytes 1732
  352.0 40.6 %copy-start.22 = (f32[144]{0:T(256)S(1)}, f32[144]{0:T(256)}, u32[]{:S(2)}) copy-start(f32[144]{0:T(256)} %param.39) | copy-start | bytes 1732
  352.0 41.2 %copy-start.5 = (f32[144,960]{1,0:T(8,128)S(1)}, f32[144,960]{1,0:T(8,128)}, u32[]{:S(2)}) copy-start(f32[144,960]{1,0:T(8,128)} %param.25) | copy-start | bytes 1658884
  352.0 41.2 %copy-start.11 = (f32[144,960]{1,0:T(8,128)S(1)}, f32[144,960]{1,0:T(8,128)}, u32[]{:S(2)}) copy-start(f32[144,960]{1,0:T(8,128)} %param.31) | copy-start | bytes 1658884
  352.0 41.1 %copy-start.12 = (f32[144,960]{1,0:T(8,128)S(1)}, f32[144,960]{1,0:T(8,128)}, u32[]{:S(2)}) copy-start(f32[144,960]{1,0:T(8,128)} %param.37) | copy-start | bytes 1658884
  353.1 42.6 %collective-permute-start.11 = (bf16[512,576]{0,1:T(8,128)(2,1)}, bf16[512,576]{0,1:T(8,128)(2,1)}, u32[]{:S(2)}, u32[]{:S(2)}) collective-permute-start(bf16[512,576]{0,1:T(8,128)(2,1)} %copy.116), channel_id=1, source_target_pairs={{0,0},{4,1},{5,2},{1,3},{2,4},{6,5},{7,6},{3,7},{8,8},{12,9},{13,1... | collective-permute-start | bytes 1769480 | tf_op jit(solution)/shard_map/ppermute | solution.py:762
  391.9 3.8 copy-start.13
  391.9 3.8 copy-start.14

commit v2 on v1

v2 whole, which is shorter than its diff:
```python
import functools

import jax
import jax.numpy as jnp
import numpy as np
from jax import lax
from jax.experimental import pallas as pl
from jax.experimental.pallas import tpu as pltpu
from jax.sharding import PartitionSpec as P

HEADS = 9
KV_HEADS = 3
HEAD_DIM = 64
HALF = HEAD_DIM // 2
GROUP = HEADS // KV_HEADS
STEP = 2

norm_eps = 1e-05
rope_base = 100000.0
beta_one = 0.9
beta_two = 0.95
adam_eps = 1e-08
learn_rate = 0.2
decay_rate = 0.1

bf16 = jnp.bfloat16
f32 = jnp.float32
NEG = -1e30
NN = (((1,), (0,)), ((), ()))
NT = (((1,), (1,)), ((), ()))
MESH = pl.DeviceIdType.MESH
VMEM = pl.BlockSpec(memory_space=pltpu.VMEM)
HBM = pl.BlockSpec(memory_space=pl.ANY)


def dot(left, right, dims=NN):
    return lax.dot_general(left, right, dims, preferred_element_type=f32)


class Place:
    def __init__(self):
        dp = lax.axis_index("dp")
        self.base = (dp // 8) * 8
        self.chip = (dp % 8) // 2
        self.core = dp % 2
        self.z = lax.axis_index("seq")

    def at(self, chip, core, z):
        return {"dp": self.base + 2 * chip + core, "seq": z}

    def sibling(self):
        return self.at(self.chip, 1 - self.core, self.z)

    def meet(self):
        barrier = pltpu.get_barrier_semaphore()
        for r in range(4):
            for c in range(2):
                if r + c > 0:
                    pl.semaphore_signal(
                        barrier,
                        inc=1,
                        device_id=self.at(self.chip, (self.core + c) % 2, (self.z + r) % 4),
                        device_id_type=MESH,
                    )
        for r in range(1, 4):
            pl.semaphore_signal(
                barrier,
                inc=1,
                device_id=self.at((self.chip + r) % 4, self.core, self.z),
                device_id_type=MESH,
            )
        return barrier

    def met(self, barrier):
        pl.semaphore_wait(barrier, 10)


def remote(src, dst, send_sem, recv_sem, target):
    return pltpu.make_async_remote_copy(
        src_ref=src,
        dst_ref=dst,
        send_sem=send_sem,
        recv_sem=recv_sem,
        device_id=target,
        device_id_type=MESH,
    )


class Exchange:
    def __init__(self, place, src, dst, sems, row, forward):
        self.place, self.src, self.dst, self.row = place, src, dst, row
        self.local, self.sent, self.got = sems
        z, core = place.z, place.core
        taker = ((z + 1) // 2) % 2
        if forward:
            self.goes = [(2 * core + i, taker) for i in range(2)]
            self.comes = [(core if i == 0 else 3 - core, z // 2) for i in range(2)]
            self.slot = z // 2
        else:
            self.goes = [(core if i == 0 else 3 - core, z // 2) for i in range(2)]
            self.comes = [(2 * core + i, taker) for i in range(2)]
            self.slot = z % 2

    def same(self, spot):
        return (spot[0] == self.place.z) & (spot[1] == self.place.core)

    def far(self, i):
        z, core = self.goes[i]
        return remote(
            self.src.at[i],
            self.dst.at[self.slot],
            self.sent.at[self.row, i],
            self.got.at[self.row, self.slot],
            self.place.at(self.place.chip, core, z),
        )

    def near(self, i):
        return pltpu.make_async_copy(
            self.src.at[i], self.dst.at[self.slot], self.local.at[self.row, i]
        )

    def start(self, i):
        @pl.when(self.same(self.goes[i]))
        def _():
            self.near(i).start()

        @pl.when(jnp.logical_not(self.same(self.goes[i])))
        def _():
            self.far(i).start()

    def arrive(self, i):
        @pl.when(jnp.logical_not(self.same(self.comes[i])))
        def _():
            remote(
                self.dst.at[i],
                self.dst.at[i],
                self.sent.at[self.row, i],
                self.got.at[self.row, i],
                self.place.sibling(),
            ).wait_recv()

    def near_done(self, i):
        @pl.when(self.same(self.goes[i]))
        def _():
            self.near(i).wait()

    def far_done(self, i):
        @pl.when(jnp.logical_not(self.same(self.goes[i])))
        def _():
            self.far(i).wait_send()


class Gather:
    def __init__(self, place, part, full, by_rows, sems, row):
        self.place, self.part, self.full, self.by_rows = place, part, full, by_rows
        self.local, self.sent, self.got = sems
        self.row = row
        self.rows = part.shape[0]
        self.size = (part.shape[0] if by_rows else part.shape[1]) // 8
        self.mine = 2 * place.chip + place.core

    def window(self, which, quarter):
        if self.by_rows:
            start = quarter * self.rows + which * self.size
            return (pl.ds(pl.multiple_of(start, 16), self.size), slice(None))
        return (
            pl.ds(pl.multiple_of(quarter * self.rows, 16), self.rows),
            pl.ds(pl.multiple_of(which * self.size, 128), self.size),
        )

    def copy(self, src, dst, slot, target):
        return remote(src, dst, self.sent.at[self.row, slot], self.got.at[self.row, slot], target)

    def own(self):
        start = pl.multiple_of(self.place.z * self.rows, 16)
        return pltpu.make_async_copy(
            self.part, self.full.at[pl.ds(start, self.rows), :], self.local.at[self.row]
        )

    def over_z(self, r):
        here = self.place
        return self.copy(
            self.part.at[self.window(self.mine, 0)],
            self.full.at[self.window(self.mine, here.z)],
            r - 1,
            here.at(here.chip, here.core, (here.z + r) % 4),
        )

    def spread(self, r):
        here = self.place
        ref = self.full.at[self.window(self.mine, (here.z + 4 - r) % 4)]
        copies = [
            self.copy(
                ref, ref, 3 * r + s - 1, here.at((here.chip + s) % 4, here.core, here.z)
            )
            for s in range(1, 4)
        ]
        return copies + [self.copy(ref, ref, 11 + r, here.sibling())]

    def hand_on(self, r, s):
        here = self.place
        which = 2 * ((here.chip + 4 - s) % 4) + here.core
        ref = self.full.at[self.window(which, (here.z + 4 - r) % 4)]
        return self.copy(ref, ref, 15 + 3 * (r - 1) + s - 1, here.sibling())

    def landed(self, which, r, slot):
        ref = self.full.at[self.window(which, (self.place.z + 4 - r) % 4)]
        self.copy(ref, ref, slot, self.place.sibling()).wait_recv()

    def first(self):
        self.own().start()
        for r in range(1, 4):
            self.over_z(r).start()

    def second(self):
        for r in range(1, 4):
            self.landed(self.mine, r, r - 1)
            for item in self.spread(r):
                item.start()

    def third(self):
        for r in range(1, 4):
            for s in range(1, 4):
                which = 2 * ((self.place.chip + 4 - s) % 4) + self.place.core
                self.landed(which, r, 3 * r + s - 1)
                self.hand_on(r, s).start()

    def finish(self):
        chip, other = self.place.chip, 1 - self.place.core
        for r in range(1, 4):
            self.landed(2 * chip + other, r, 11 + r)
            for s in range(1, 4):
                which = 2 * ((chip + 4 - s) % 4) + other
                self.landed(which, r, 15 + 3 * (r - 1) + s - 1)
        self.own().wait()

    def drain(self):
        for r in range(1, 4):
            self.over_z(r).wait_send()
            for item in self.spread(r):
                item.wait_send()
            for s in range(1, 4):
                self.hand_on(r, s).wait_send()


class Scatter:
    def __init__(self, place, grad, out, by_rows, scratch, sems, row):
        self.place, self.grad, self.out, self.by_rows = place, grad, out, by_rows
        self.mine_s, self.r0, self.r1, self.r2 = scratch
        self.local, self.sent, self.got = sems
        self.row = row
        self.size = (out.shape[0] if by_rows else out.shape[1]) // 8

    def block(self, which):
        if self.by_rows:
            return (pl.ds(pl.multiple_of(which * self.size, 16), self.size), slice(None))
        return (slice(None), pl.ds(pl.multiple_of(which * self.size, 128), self.size))

    def copy(self, src, dst, slot, target):
        return remote(src, dst, self.sent.at[self.row, slot], self.got.at[self.row, slot], target)

    def landed(self, ref, slot):
        self.copy(ref, ref, slot, self.place.sibling()).wait_recv()

    def own(self, s):
        here = self.place
        which = 2 * ((here.chip + s) % 4) + here.core
        return pltpu.make_async_copy(
            self.grad.at[(slice(None),) + self.block(which)],
            self.mine_s.at[s],
            self.local.at[self.row, s],
        )

    def to_sibling(self, s):
        here = self.place
        which = 2 * ((here.chip + s) % 4) + 1 - here.core
        return self.copy(
            self.grad.at[(slice(None),) + self.block(which)], self.r0.at[s], s, here.sibling()
        )

    def to_chip(self, s):
        here = self.place
        return self.copy(
            self.mine_s.at[s],
            self.r1.at[s - 1],
            3 + s,
            here.at((here.chip + s) % 4, here.core, here.z),
        )

    def to_z(self, r):
        here = self.place
        return self.copy(
            self.mine_s.at[0, (here.z + r) % 4],
            self.r2.at[r - 1],
            6 + r,
            here.at(here.chip, here.core, (here.z + r) % 4),
        )

    def spread(self):
        here = self.place
        ref = self.out.at[self.block(2 * here.chip + here.core)]
        copies = [
            self.copy(ref, ref, 9 + s, here.at((here.chip + s) % 4, here.core, here.z))
            for s in range(1, 4)
        ]
        return copies + [self.copy(ref, ref, 13, here.sibling())]

    def hand_on(self, s):
        here = self.place
        ref = self.out.at[self.block(2 * ((here.chip + 4 - s) % 4) + here.core)]
        return self.copy(ref, ref, 13 + s, here.sibling())

    def start(self):
        for s in (1, 2, 3, 0):
            self.to_sibling(s).start()
            self.own(s).start()

    def pair(self):
        for s in (1, 2, 3, 0):
            self.own(s).wait()
            self.landed(self.r0.at[s], s)
            total = self.mine_s[s].astype(f32) + self.r0[s].astype(f32)
            self.mine_s[s] = total.astype(bf16)
            if s > 0:
                self.to_chip(s).start()

    def plane(self):
        for s in range(1, 4):
            self.landed(self.r1.at[s - 1], 3 + s)
        total = self.mine_s[0].astype(f32)
        for s in range(1, 4):
            total = total + self.r1[s - 1].astype(f32)
        self.mine_s[0] = total.astype(bf16)
        for r in range(1, 4):
            self.to_z(r).start()

    def line(self):
        for r in range(1, 4):
            self.landed(self.r2.at[r - 1], 6 + r)
        total = self.mine_s[0, self.place.z].astype(f32)
        for r in range(1, 4):
            total = total + self.r2[r - 1].astype(f32)
        self.out[self.block(2 * self.place.chip + self.place.core)] = total.astype(bf16)
        for item in self.spread():
            item.start()

    def share(self):
        for s in range(1, 4):
            which = 2 * ((self.place.chip + 4 - s) % 4) + self.place.core
            self.landed(self.out.at[self.block(which)], 9 + s)
            self.hand_on(s).start()

    def finish(self):
        chip, other = self.place.chip, 1 - self.place.core
        self.landed(self.out.at[self.block(2 * chip + other)], 13)
        for s in range(1, 4):
            which = 2 * ((chip + 4 - s) % 4) + other
            self.landed(self.out.at[self.block(which)], 13 + s)

    def drain(self):
        for s in range(4):
            self.to_sibling(s).wait_send()
        for s in range(1, 4):
            self.to_chip(s).wait_send()
            self.to_z(s).wait_send()
            self.hand_on(s).wait_send()
        for item in self.spread():
            item.wait_send()


def scatter_part(array, by_rows):
    rows = array.shape[0] // 4
    return (4, rows // 8, array.shape[1]) if by_rows else (4, rows, array.shape[1] // 8)


def scatter_scratch(part):
    return [
        pltpu.VMEM((4,) + part, bf16),
        pltpu.VMEM((4,) + part, bf16),
        pltpu.VMEM((3,) + part, bf16),
        pltpu.VMEM((3,) + part[1:], bf16),
    ]


def column_row(tile, lane, height):
    return tile.astype(f32).T[lane : lane + 1, :]


def visible(key_start, keys, lows, first_query, own, causal):
    size = lows.shape[1]
    shape = (keys, size - first_query)
    key = lax.broadcasted_iota(jnp.int32, shape, 0) + key_start
    seen = key >= lows[:, first_query:]
    if causal:
        query = lax.broadcasted_iota(jnp.int32, shape, 1) + (own + first_query)
        seen = seen & (key <= query)
    return seen


def front_kernel(
    tokens, positions, cotangent, turns, balance, projector, combiner, leveler, expander,
    reducer, x_ref, dy_ref, q_ref, kv, o_ref, lse_ref, cos_ref, sin_ref, low_ref, proj, wide, down,
    keys, pos, proj_part, wide_part, down_part,
    ex_local, ex_sent, ex_got, ga_local, ga_sent, ga_got, kv_sent, kv_got,
):
    here = Place()
    core = here.core
    chunk = q_ref.shape[3]
    half = chunk // 2
    model = x_ref.shape[2]
    rows, width = projector.shape
    inner = combiner.shape[1]
    hidden2 = expander.shape[1]
    barrier = here.meet()

    def column(vector):
        return jnp.broadcast_to(vector[...], (128, rows)).T

    def pack(part, pieces, gain):
        at = 0
        for piece in pieces[:-1]:
            part[:, at : at + piece.shape[1]] = piece[...].astype(bf16)
            at += piece.shape[1]
        last = pieces[-1]
        cut = last.shape[1] // 128 * 128
        part[:, at : at + cut] = last[:, :cut].astype(bf16)
        rest = last.shape[1] - cut
        end = part.shape[1] - at - cut - 128
        tail = [last[:, cut:], column(gain)[:, : 128 - rest]]
        if end > 0:
            tail.append(jnp.zeros((rows, end), f32))
        part[:, at + cut :] = jnp.concatenate(tail, axis=1).astype(bf16)

    pack(proj_part, [projector], balance)
    here.met(barrier)
    ga = (ga_local, ga_sent, ga_got)
    ex = (ex_local, ex_sent, ex_got)
    proj_in = Gather(here, proj_part, proj, False, ga, 0)
    wide_in = Gather(here, wide_part, wide, False, ga, 1)
    down_in = Gather(here, down_part, down, True, ga, 2)
    pos_in = Exchange(here, positions, pos, ex, 0, True)
    x_in = Exchange(here, tokens, x_ref, ex, 1, True)
    dy_in = Exchange(here, cotangent, dy_ref, ex, 2, True)
    proj_in.first()
    for i in range(2):
        pos_in.start(i)
    for i in range(2):
        x_in.start(i)
    pack(wide_part, [expander, combiner], leveler)
    down_part[...] = reducer[...].astype(bf16)

    for i in range(2):
        pos_in.near_done(i)
    for i in range(2):
        pos_in.arrive(i)
    inverse = jnp.concatenate([turns[...]] * (chunk // 128), axis=1)
    for s in range(2):
        row = jnp.concatenate([pos[s, i : i + 1, :] for i in range(chunk // 128)], axis=1)
        phases = row.astype(f32) * inverse
        cos_ref[s] = jnp.cos(phases)
        sin_ref[s] = jnp.sin(phases)
        start = (core if s == 0 else 3 - core) * chunk
        low_ref[s] = lax.broadcasted_iota(jnp.int32, (1, chunk), 1) + start - row

    proj_in.second()
    proj_in.third()
    proj_in.finish()
    tile = width // 128 * 128
    gain = column_row(proj[:, tile : tile + 128], width - tile, model)
    w_t = proj[...].T[:width, :]

    def kv_copy(s):
        mine = core if s == 0 else 3 - core
        return remote(
            kv.at[mine], kv.at[mine], kv_sent.at[s], kv_got.at[s], here.sibling()
        )

    for i in range(2):
        x_in.near_done(i)
    for s in range(2):
        x_in.arrive(s)
        if s == 1:
            wide_in.first()
            down_in.first()
            for i in range(2):
                dy_in.start(i)
        x = x_ref[s].astype(f32)
        rho = lax.rsqrt(jnp.mean(x * x, axis=1, keepdims=True) + norm_eps)
        a = (x * rho * gain).astype(bf16)
        zs = dot(w_t, a, NT)
        cos = cos_ref[s]
        sin = sin_ref[s]
        mine = core if s == 0 else 3 - core

        def rotated(head):
            u1 = zs[head * HEAD_DIM : head * HEAD_DIM + HALF]
            u2 = zs[head * HEAD_DIM + HALF : (head + 1) * HEAD_DIM]
            return jnp.concatenate([u1 * cos - u2 * sin, u2 * cos + u1 * sin], axis=0).astype(bf16)

        for head in range(KV_HEADS):
            kv[mine, head] = rotated(HEADS + head)
            low = inner + (KV_HEADS + head) * HEAD_DIM
            kv[mine, KV_HEADS + head] = zs[low : low + HEAD_DIM].astype(bf16)
        kv_copy(s).start()
        for head in range(HEADS):
            q_ref[s, head] = rotated(head) * jnp.asarray(0.125, bf16)
    for s in range(2):
        theirs = 1 - core if s == 0 else 2 + core
        remote(
            kv.at[theirs], kv.at[theirs], kv_sent.at[s], kv_got.at[s], here.sibling()
        ).wait_recv()
    for s in range(2):
        kv_copy(s).wait_send()

    for c in range(4):
        for g in range(KV_HEADS):
            keys[c, g] = kv[c, g].T

    def outer(step, carry):
        g = step // 2
        s = step % 2
        mine = core + s * (3 - 2 * core)
        lows = low_ref[s]
        qs = [q_ref[s, GROUP * g + j] for j in range(GROUP)]

        @pl.when(step == 2)
        def _():
            wide_in.second()
            down_in.second()

        def scores(c, k0, n, q0, causal):
            key_rows = keys[c, g, k0 : k0 + n, :]
            seen = visible(c * chunk + k0, n, lows, q0, mine * chunk, causal)
            raw = [dot(key_rows, q[:, q0:]) for q in qs]
            return [jnp.where(seen, r, NEG) for r in raw]

        def update(c, k0, n, masked, state):
            vals = kv[c, KV_HEADS + g, :, k0 : k0 + n]
            tops = [jnp.max(m, axis=0, keepdims=True) for m in masked]
            if state is not None:
                tops = [jnp.maximum(old[0], top) for old, top in zip(state, tops)]
            probs = [jnp.exp(m - top) for m, top in zip(masked, tops)]
            lows_ = [p.astype(bf16) for p in probs]
            sums = [jnp.sum(p, axis=0, keepdims=True) for p in probs]
            mixes = [dot(vals, p) for p in lows_]
            if state is None:
                return tuple(zip(tops, sums, mixes))
            new = []
            for old, top, total, mix in zip(state, tops, sums, mixes):
                shrink = jnp.exp(old[0] - top)
                new.append((top, old[1] * shrink + total, old[2] * shrink + mix))
            return tuple(new)

        early = scores(mine, 0, half, 0, True)
        late = scores(mine, half, half, half, True)
        first = update(mine, 0, half, early, None)
        second = update(
            mine, half, half, late, [tuple(part[:, half:] for part in item) for item in first]
        )
        state = tuple(
            tuple(jnp.concatenate([a[:, :half], b], axis=1) for a, b in zip(one, two))
            for one, two in zip(first, second)
        )
        state = lax.fori_loop(
            0,
            mine,
            lambda c, now: update(c, 0, chunk, scores(c, 0, chunk, 0, False), now),
            state,
        )
        for j in range(GROUP):
            top, total, mix = state[j]
            o_ref[s, GROUP * g + j] = (mix / total).astype(bf16)
            lse_ref[s, GROUP * g + j] = top + jnp.log(total)
        return carry

    lax.fori_loop(0, 2 * KV_HEADS, outer, 0)
    for item in (wide_in, down_in):
        item.third()
    for i in range(2):
        dy_in.near_done(i)
        dy_in.arrive(i)
    for item in (wide_in, down_in):
        item.finish()
    for item in (proj_in, wide_in, down_in):
        item.drain()
    for item in (pos_in, x_in, dy_in):
        for i in range(2):
            item.far_done(i)


def front(tokens, positions, cotangent, weights):
    _, chunk, model = tokens.shape
    rows, width = weights[1].shape
    hidden = weights[5].shape[0]
    sd = jax.ShapeDtypeStruct
    exponent = np.arange(HALF, dtype=np.float32) * np.float32(2.0 / HEAD_DIM)
    turns = np.power(np.float32(rope_base), -exponent).astype(np.float32)
    turns = jnp.asarray(np.broadcast_to(turns[:, None], (HALF, 128)))
    outs = [
        (sd(tokens.shape, bf16), VMEM),
        (sd(tokens.shape, bf16), HBM),
        (sd((2, HEADS, HEAD_DIM, chunk), bf16), VMEM),
        (sd((4, 2 * KV_HEADS, HEAD_DIM, chunk), bf16), VMEM),
        (sd((2, HEADS, HEAD_DIM, chunk), bf16), VMEM),
        (sd((2, HEADS, 1, chunk), f32), VMEM),
        (sd((2, HALF, chunk), f32), VMEM),
        (sd((2, HALF, chunk), f32), VMEM),
        (sd((2, 1, chunk), jnp.int32), VMEM),
        (sd((4 * rows, 1024), bf16), VMEM),
        (sd((4 * rows, 4096), bf16), HBM),
        (sd((4 * hidden, model), bf16), HBM),
    ]
    return pl.pallas_call(
        front_kernel,
        out_shape=[shape for shape, _ in outs],
        in_specs=[HBM, VMEM, HBM] + [VMEM] * 7,
        out_specs=[spec for _, spec in outs],
        scratch_shapes=[
            pltpu.VMEM((4, KV_HEADS, chunk, HEAD_DIM), bf16),
            pltpu.VMEM((2, chunk // 128, 128), jnp.int32),
            pltpu.VMEM((rows, 1024), bf16),
            pltpu.VMEM((rows, 4096), bf16),
            pltpu.VMEM((hidden, model), bf16),
            pltpu.SemaphoreType.DMA((3, 2)),
            pltpu.SemaphoreType.DMA((3, 2)),
            pltpu.SemaphoreType.DMA((3, 2)),
            pltpu.SemaphoreType.DMA((3,)),
            pltpu.SemaphoreType.DMA((3, 24)),
            pltpu.SemaphoreType.DMA((3, 24)),
            pltpu.SemaphoreType.DMA((2,)),
            pltpu.SemaphoreType.DMA((2,)),
        ],
        compiler_params=pltpu.CompilerParams(
            collective_id=0, has_side_effects=True, vmem_limit_bytes=58 << 20
        ),
    )(tokens, positions.reshape(2, chunk // 128, 128), cotangent, turns, *weights)


def feed_kernel(
    x_ref, o_ref, dy_ref, wide_ref, down_ref, out_ref, dm_ref, do_ref, gwide_ref, gdown_ref,
    act_s, dgu_s, a_s, dm_s, gain_s,
):
    rows_all, model = x_ref.shape
    hidden = down_ref.shape[0]
    inner = o_ref.shape[1]
    block = 256
    per = o_ref.shape[2] // block
    comb0 = 2 * hidden
    tile = (comb0 + model) // 128 * 128
    lane = comb0 + model - tile
    gain = column_row(wide_ref[:, tile : tile + 128], lane, model)
    gain_s[...] = jnp.zeros_like(gain_s)
    pieces = 3
    size = hidden // pieces

    def one(t, carry):
        rows = pl.ds(pl.multiple_of(t * block, block), block)
        cols = pl.ds(pl.multiple_of((t % per) * block, block), block)
        comb = wide_ref[:, comb0 : comb0 + model]
        m = x_ref[rows, :].astype(f32) + dot(o_ref[t // per, :, cols].T, comb)
        rho = lax.rsqrt(jnp.mean(m * m, axis=1, keepdims=True) + norm_eps)
        n = m * rho
        a = (n * gain).astype(bf16)
        a_s[rows, :] = a
        dy = dy_ref[rows, :]
        total = m
        da = None
        for f in range(pieces):
            low, high = f * size, (f + 1) * size
            w_g = wide_ref[:, low:high]
            w_u = wide_ref[:, hidden + low : hidden + high]
            w_d = down_ref[low:high, :]
            g = dot(a, w_g)
            u = dot(a, w_u)
            dact = dot(dy, w_d, NT)
            sig = 0.5 * jnp.tanh(0.5 * g) + 0.5
            silu = g * sig
            act = (silu * u).astype(bf16)
            du = (dact * silu).astype(bf16)
            dg = (dact * u * (sig + silu * (1.0 - sig))).astype(bf16)
            act_s[rows, low:high] = act
            dgu_s[rows, low:high] = dg
            dgu_s[rows, hidden + low : hidden + high] = du
            total = total + dot(act, w_d)
            part = dot(dg, w_g, NT) + dot(du, w_u, NT)
            da = part if da is None else da + part
        out_ref[rows, :] = total.astype(bf16)
        gain_s[...] += jnp.sum(da * n, axis=0, keepdims=True)
        dn = da * gain
        dm = dy.astype(f32) + rho * (dn - n * jnp.mean(dn * n, axis=1, keepdims=True))
        dm_ref[rows, :] = dm
        dm_low = dm.astype(bf16)
        dm_s[rows, :] = dm_low
        do_ref[t // per, :, cols] = dot(comb, dm_low, NT).astype(bf16)
        return carry

    lax.fori_loop(0, rows_all // block, one, 0)
    rows_d = 384

    def down_grad(i, carry):
        rows = pl.ds(pl.multiple_of(i * rows_d, 128), rows_d)
        gdown_ref[rows, :] = dot(act_s[:, rows].T, dy_ref[...]).astype(bf16)
        return carry

    lax.fori_loop(0, hidden // rows_d, down_grad, 0)
    a_t = a_s[...].T
    cols_w = 512

    def wide_grad(i, carry):
        cols = pl.ds(pl.multiple_of(i * cols_w, 128), cols_w)
        gwide_ref[:, cols] = dot(a_t, dgu_s[:, cols]).astype(bf16)
        return carry

    lax.fori_loop(0, 2 * hidden // cols_w, wide_grad, 0)
    chunk = o_ref.shape[2]
    comb_grad = dot(o_ref[0], dm_s[:chunk, :]) + dot(o_ref[1], dm_s[chunk:, :])
    gain_col = jnp.broadcast_to(gain_s[...], (128, model)).T
    end = gwide_ref.shape[1]
    gwide_ref[:, comb0:tile] = comb_grad[:, : tile - comb0].astype(bf16)
    gwide_ref[:, tile:end] = jnp.concatenate(
        [
            comb_grad[:, tile - comb0 :],
            gain_col[:, : 128 - lane],
            jnp.zeros((inner, end - tile - 128), f32),
        ],
        axis=1,
    ).astype(bf16)


def feed(x, o, dy, wide, down):
    rows, model = x.shape
    hidden = down.shape[0]
    return pl.pallas_call(
        feed_kernel,
        out_shape=[
            jax.ShapeDtypeStruct((rows, model), bf16),
            jax.ShapeDtypeStruct((rows, model), f32),
            jax.ShapeDtypeStruct(o.shape, bf16),
            jax.ShapeDtypeStruct(wide.shape, bf16),
            jax.ShapeDtypeStruct(down.shape, bf16),
        ],
        in_specs=[VMEM] * 5,
        out_specs=[VMEM] * 5,
        scratch_shapes=[
            pltpu.VMEM((rows, hidden), bf16),
            pltpu.VMEM((rows, 2 * hidden), bf16),
            pltpu.VMEM((rows, model), bf16),
            pltpu.VMEM((rows, model), bf16),
            pltpu.VMEM((1, model), f32),
        ],
        compiler_params=pltpu.CompilerParams(vmem_limit_bytes=60 << 20),
    )(x, o, dy, wide, down)


def back_kernel(
    inner,
    q_ref, kv, o_ref, lse_ref, do_ref, cos_ref, sin_ref, low_ref, x_any, dm_any, proj_any,
    gwide, gdown, out_any,
    layer_ref, dx_ref, swide, sdown, sproj,
    keys, values, dkv, dq, dq_now, give, take, x_ref, dm_ref, proj, dx_s, gproj,
    wide_a, wide_b, wide_c, wide_d, down_a, down_b, down_c, down_d,
    proj_a, proj_b, proj_c, proj_d,
    load, ex_local, ex_sent, ex_got, sc_local, sc_sent, sc_got, kv_sent, kv_got,
):
    here = Place()
    core = here.core
    chunk = q_ref.shape[3]
    half = chunk // 2
    model = x_ref.shape[2]
    width = inner + 2 * KV_HEADS * HEAD_DIM
    barrier = here.meet()
    loads = [
        pltpu.make_async_copy(src, dst, load.at[i])
        for i, (src, dst) in enumerate(((x_any, x_ref), (dm_any, dm_ref), (proj_any, proj)))
    ]
    for item in loads:
        item.start()
    here.met(barrier)
    sc = (sc_local, sc_sent, sc_got)
    ex = (ex_local, ex_sent, ex_got)
    down_sum = Scatter(here, gdown, sdown, True, (down_a, down_b, down_c, down_d), sc, 0)
    wide_sum = Scatter(here, gwide, swide, False, (wide_a, wide_b, wide_c, wide_d), sc, 1)
    proj_sum = Scatter(here, gproj, sproj, False, (proj_a, proj_b, proj_c, proj_d), sc, 2)
    out_back = Exchange(here, out_any, layer_ref, ex, 0, False)
    dx_back = Exchange(here, dx_s, dx_ref, ex, 1, False)
    down_sum.start()
    wide_sum.start()
    for i in range(2):
        out_back.start(i)

    for c in range(4):
        for g in range(KV_HEADS):
            keys[c, g] = kv[c, g].T
            values[c, g] = kv[c, KV_HEADS + g].T
        for g in range(2 * KV_HEADS):
            dkv[c, g] = jnp.zeros((HEAD_DIM, chunk), f32)

    def outer(step, carry):
        g = step // 2
        s = step % 2
        mine = core + s * (3 - 2 * core)
        lows = low_ref[s]

        @pl.when(step == 1)
        def _():
            down_sum.pair()

        @pl.when(step == 2)
        def _():
            wide_sum.pair()

        @pl.when(step == 4)
        def _():
            down_sum.plane()

        @pl.when(step == 5)
        def _():
            down_sum.line()

        qs = [q_ref[s, GROUP * g + j] for j in range(GROUP)]
        dos = [do_ref[s, GROUP * g + j] for j in range(GROUP)]
        lses = [lse_ref[s, GROUP * g + j] for j in range(GROUP)]
        deltas = [
            jnp.sum(
                dos[j].astype(f32) * o_ref[s, GROUP * g + j].astype(f32), axis=0, keepdims=True
            )
            for j in range(GROUP)
        ]

        def block(c, k0, n, q0, causal):
            key_rows = keys[c, g, k0 : k0 + n, :]
            value_rows = values[c, g, k0 : k0 + n, :]
            key_cols = kv[c, g, :, k0 : k0 + n]
            seen = visible(c * chunk + k0, n, lows, q0, mine * chunk, causal)
            raw = [dot(key_rows, q[:, q0:]) for q in qs]
            dps = [dot(value_rows, d[:, q0:]) for d in dos]
            probs = [
                jnp.exp(jnp.where(seen, r, NEG) - lse[:, q0:]) for r, lse in zip(raw, lses)
            ]
            lows_ = [p.astype(bf16) for p in probs]
            dss = [
                (p * (dp - delta[:, q0:])).astype(bf16)
                for p, dp, delta in zip(probs, dps, deltas)
            ]
            dkv[c, KV_HEADS + g, :, k0 : k0 + n] += dot(
                jnp.concatenate([d[:, q0:] for d in dos], axis=1),
                jnp.concatenate(lows_, axis=1),
                NT,
            )
            dkv[c, g, :, k0 : k0 + n] += dot(
                jnp.concatenate([q[:, q0:] for q in qs], axis=1),
                jnp.concatenate(dss, axis=1),
                NT,
            )
            return [dot(key_cols, ds) for ds in dss]

        early = block(mine, 0, half, 0, True)
        late = block(mine, half, half, half, True)
        for j in range(GROUP):
            dq_now[j] = jnp.concatenate(
                [early[j][:, :half], early[j][:, half:] + late[j]], axis=1
            )

        def more(c, carry_in):
            extra = block(c, 0, chunk, 0, False)
            for j in range(GROUP):
                dq_now[j] += extra[j]
            return carry_in

        lax.fori_loop(0, mine, more, 0)
        for j in range(GROUP):
            dq[s, GROUP * g + j] = 0.125 * dq_now[j]
        return carry

    lax.fori_loop(0, 2 * KV_HEADS, outer, 0)

    def give_copy(s):
        return remote(give.at[s], take.at[s], kv_sent.at[s], kv_got.at[s], here.sibling())

    for s in range(2):
        theirs = 1 - core if s == 0 else 2 + core
        give[s] = dkv[theirs].astype(bf16)
        give_copy(s).start()
    for item in loads:
        item.wait()
    tile = width // 128 * 128
    lane = width - tile
    gain = column_row(proj[:, tile : tile + 128], lane, model)
    w = proj[:, :width]
    grad = None
    gain_grad = None
    for s in range(2):
        cos = cos_ref[s]
        sin = sin_ref[s]
        mine = core if s == 0 else 3 - core

        def turned(d):
            d1 = d[:HALF]
            d2 = d[HALF:]
            return jnp.concatenate([d1 * cos + d2 * sin, d2 * cos - d1 * sin], axis=0)

        give_copy(s).wait_recv()
        parts = [turned(dq[s, head]) for head in range(HEADS)]
        full = [dkv[mine, head] + take[s, head].astype(f32) for head in range(2 * KV_HEADS)]
        parts += [turned(full[head]) for head in range(KV_HEADS)]
        parts += full[KV_HEADS:]
        dz_t = jnp.concatenate([part.astype(bf16) for part in parts], axis=0)
        x = x_ref[s].astype(f32)
        rho = lax.rsqrt(jnp.mean(x * x, axis=1, keepdims=True) + norm_eps)
        n = x * rho
        a = (n * gain).astype(bf16)
        da = dot(dz_t.T, w, NT)
        dn = da * gain
        dx = dm_ref[s] + rho * (dn - n * jnp.mean(dn * n, axis=1, keepdims=True))
        dx_s[s] = dx.astype(bf16)
        dx_back.start(s)
        part = dot(a.T, dz_t, NT)
        grad = part if grad is None else grad + part
        part = jnp.sum(da * n, axis=0, keepdims=True)
        gain_grad = part if gain_grad is None else gain_grad + part
    gain_col = jnp.broadcast_to(gain_grad, (128, model)).T
    full = jnp.concatenate([grad, gain_col[:, : sproj.shape[1] - width]], axis=1).astype(bf16)
    rows = model // 4
    for quarter in range(4):
        gproj[quarter] = full[quarter * rows : (quarter + 1) * rows, :]
    proj_sum.start()
    wide_sum.plane()
    proj_sum.pair()
    down_sum.share()
    wide_sum.line()
    proj_sum.plane()
    wide_sum.share()
    proj_sum.line()
    proj_sum.share()
    for item in (down_sum, wide_sum, proj_sum):
        item.finish()
        item.drain()
    for item in (out_back, dx_back):
        for i in range(2):
            item.near_done(i)
            item.arrive(i)
            item.far_done(i)
    for s in range(2):
        give_copy(s).wait_send()


def back(q, kv, o, lse, do, cos, sin, lows, x, dm, proj, gwide, gdown, out):
    chunk = q.shape[3]
    model = x.shape[2]
    inner = HEADS * HEAD_DIM
    sd = jax.ShapeDtypeStruct
    wide_rows, down_rows = gwide.shape[0] // 4, gdown.shape[0] // 4
    scratch = [
        pltpu.VMEM((4, KV_HEADS, chunk, HEAD_DIM), bf16),
        pltpu.VMEM((4, KV_HEADS, chunk, HEAD_DIM), bf16),
        pltpu.VMEM((4, 2 * KV_HEADS, HEAD_DIM, chunk), f32),
        pltpu.VMEM((2, HEADS, HEAD_DIM, chunk), f32),
        pltpu.VMEM((GROUP, HEAD_DIM, chunk), f32),
        pltpu.VMEM((2, 2 * KV_HEADS, HEAD_DIM, chunk), bf16),
        pltpu.VMEM((2, 2 * KV_HEADS, HEAD_DIM, chunk), bf16),
        pltpu.VMEM(x.shape, bf16),
        pltpu.VMEM(x.shape, f32),
        pltpu.VMEM(proj.shape, bf16),
        pltpu.VMEM(x.shape, bf16),
        pltpu.VMEM((4, proj.shape[0] // 4, proj.shape[1]), bf16),
    ]
    for array, by_rows in ((gwide, False), (gdown, True), (proj, False)):
        scratch += scatter_scratch(scatter_part(array, by_rows))
    scratch += [
        pltpu.SemaphoreType.DMA((3,)),
        pltpu.SemaphoreType.DMA((2, 2)),
        pltpu.SemaphoreType.DMA((2, 2)),
        pltpu.SemaphoreType.DMA((2, 2)),
        pltpu.SemaphoreType.DMA((3, 4)),
        pltpu.SemaphoreType.DMA((3, 17)),
        pltpu.SemaphoreType.DMA((3, 17)),
        pltpu.SemaphoreType.DMA((2,)),
        pltpu.SemaphoreType.DMA((2,)),
    ]
    return pl.pallas_call(
        functools.partial(back_kernel, inner),
        out_shape=[
            sd(x.shape, bf16),
            sd(x.shape, bf16),
            sd((wide_rows, gwide.shape[1]), bf16),
            sd((down_rows, gdown.shape[1]), bf16),
            sd((proj.shape[0] // 4, proj.shape[1]), bf16),
        ],
        in_specs=[VMEM] * 8 + [HBM] * 6,
        out_specs=[HBM, HBM, VMEM, VMEM, VMEM],
        scratch_shapes=scratch,
        compiler_params=pltpu.CompilerParams(
            collective_id=1, has_side_effects=True, vmem_limit_bytes=60 << 20
        ),
    )(
        q, kv, o, lse, do, cos, sin, lows, x, dm, proj,
        gwide.reshape(4, wide_rows, gwide.shape[1]),
        gdown.reshape(4, down_rows, gdown.shape[1]),
        out,
    )


def adam_values(master, grad, mean, square, decays):
    mean_new = beta_one * mean + (1.0 - beta_one) * grad
    square_new = beta_two * square + (1.0 - beta_two) * grad * grad
    mean_hat = mean_new / (1.0 - beta_one**STEP)
    square_hat = square_new / (1.0 - beta_two**STEP)
    change = mean_hat / (jnp.sqrt(square_hat) + adam_eps)
    if decays:
        change = change + decay_rate * master
    return master - learn_rate * change, mean_new, square_new


def adam_kernel(decay_flags, swide, sdown, sproj, *refs):
    masters, means, squares = refs[:6], refs[6:12], refs[12:18]
    totals, nexts, new_means, new_squares = (refs[18 + 6 * k : 24 + 6 * k] for k in range(4))
    width = masters[1].shape[1]
    inner = masters[2].shape[1]
    hidden2 = masters[4].shape[1]

    def row_of(ref, column):
        tile = column // 128 * 128
        return column_row(ref[:, tile : tile + 128], column - tile, ref.shape[0])

    grads = (
        lambda: row_of(sproj, width),
        lambda: sproj[:, :width].astype(f32),
        lambda: swide[:, hidden2 : hidden2 + inner].astype(f32),
        lambda: row_of(swide, hidden2 + inner),
        lambda: swide[:, :hidden2].astype(f32),
        lambda: sdown[...].astype(f32),
    )
    for i in range(6):
        grad = grads[i]()
        totals[i][...] = grad
        nexts[i][...], new_means[i][...], new_squares[i][...] = adam_values(
            masters[i][...], grad, means[i][...], squares[i][...], decay_flags[i]
        )


def optimize(sums, masters, means, squares):
    decay_flags = (False, True, True, False, True, True)
    arrays = [a[None, :] if a.ndim == 1 else a for a in masters + means + squares]
    shapes = [jax.ShapeDtypeStruct(a.shape, f32) for a in arrays[:6]] * 4
    results = pl.pallas_call(
        functools.partial(adam_kernel, decay_flags),
        out_shape=shapes,
        in_specs=[VMEM] * 21,
        out_specs=[VMEM] * 24,
        compiler_params=pltpu.CompilerParams(vmem_limit_bytes=60 << 20),
    )(*sums, *arrays)
    return tuple(r.reshape(m.shape) for r, m in zip(results, masters * 4))


def on_device(tokens, positions, cotangent, *rest):
    masters, means, squares = rest[:6], rest[6:12], rest[12:18]
    dp_size = lax.axis_size("dp")
    _, chunk, model = tokens.shape
    inner = HEADS * HEAD_DIM
    weights = [a[None, :] if a.ndim == 1 else a for a in masters]
    x, dy, q, kv, o, lse, cos, sin, lows, proj, wide, down = front(
        tokens, positions, cotangent, weights
    )
    out, dm, do, gwide, gdown = feed(
        x.reshape(2 * chunk, model),
        o.reshape(2, inner, chunk),
        dy.reshape(2 * chunk, model),
        wide,
        down,
    )
    layer_out, tokens_grad, *sums = back(
        q, kv, o, lse, do.reshape(o.shape), cos, sin, lows, x, dm.reshape(x.shape), proj,
        gwide, gdown, out.reshape(x.shape),
    )
    if dp_size > 8:
        groups = [[g * 8 + k for g in range(dp_size // 8)] for k in range(8)]
        sums = [lax.psum(part, "dp", axis_index_groups=groups) for part in sums]
    return (layer_out, tokens_grad) + optimize(sums, masters, means, squares)


def solution(mesh):
    vector, matrix = P("seq"), P("seq", None)
    weights = (vector, matrix, matrix, vector, matrix, matrix)
    rows = P("dp", "seq", None)
    return jax.shard_map(
        on_device,
        mesh=mesh,
        in_specs=(rows, P("dp", "seq"), rows) + weights * 3,
        out_specs=(rows, rows) + weights * 4,
        check_vma=False,
    )
```

time: 402 us -> 291 us (0.72)
  starting transfers between devices: 48 us -> 0 us
  other arithmetic: 39 us -> 0 us
  local copies, waits for them, and re-layouts: 34.2 us -> 18.5 us
    ppermute x12 -> x0, starting transfers between devices: 48 us -> none  [the longest x5 24.5 us: swap(): lax.ppermute(one, ('dp', 'seq'), perms[0])]
    sub x7 -> x0, other arithmetic: 15.3 us -> none  [the longest x6 14.6 us: adam_step(): return (master - learn_rate * change, mean_new, square_new)]
    another operation x8 -> x0, other arithmetic: 7.93 us -> none  [the longest x7 7.86 us: unswap(): return jnp.stack([jnp.where(flip, two, one), jnp.where(flip, one, two)])]
    convert_element_type x9 -> x0, other arithmetic: 7.3 us -> none  [the longest x2 3.98 us: on_device(): swide, sdown, sproj = (part.astype(f32) for part in (swide, sdown, sproj))]
    ppermute x4 -> x0, local copies, waits for them, and re-layouts: 7 us -> none  [the longest x2 3.5 us: swap(): lax.ppermute(one, ('dp', 'seq'), perms[0])]
    select_n x6 -> x0, other arithmetic: 5.95 us -> none  [the longest x5 5.95 us: swap(): two = jnp.where(flip, pair[0], pair[1])]
    select_n x4 -> x0, local copies, waits for them, and re-layouts: 5.38 us -> none  [the longest x2 3.24 us: swap(): one = jnp.where(flip, pair[1], pair[0])]
    pallas_call x7 -> x3, Pallas kernels: 237 us -> 232 us  [the longest x1 124 us: back(): pl.pallas_call(functools.partial(back_kernel, inner), out_shape=[sd(x.sha...]
  transfers between devices with their start and end apart: 12 -> 0, of which waited for: 1 -> 0; matrix products, arithmetic and copies ran while one was open for 16% -> 0% of each run, Pallas kernels for 43% -> 0%
where the time goes in v2:
time: 291 us; the launch traced here: 289 us
  Pallas kernels  270 us (93%)
  local copies, waits for them, and re-layouts  18.5 us (6%)
    pallas_call x1, Pallas kernels, back(): pl.pallas_call(functools.partial(back_kernel, inner), out_shape=[sd(x.sha...  124 us
    pallas_call x1, Pallas kernels, front(): pl.pallas_call(front_kernel, out_shape=[shape for shape, _ in outs], in_s...  95.6 us
    pallas_call x1, Pallas kernels, feed(): pl.pallas_call(feed_kernel, out_shape=[jax.ShapeDtypeStruct((rows, model)...  37.7 us
    unnamed x33, local copies, waits for them, and re-layouts  17.3 us
    pallas_call x1, Pallas kernels, optimize(): pl.pallas_call(functools.partial(adam_kernel, decay_flags), out_shape=sha...  12.7 us

profile of v2, /device:TPU:0, one launch (start us, length us, event | category | flops | bytes accessed | tf_op | source)
XLA Modules:
  0.0 288.9 jit_solution(7163368400808132474)
XLA Ops:
  0.7 0.0 copy-start.2
  0.7 2.5 copy.50.reducer.refs_5_
  3.2 0.0 copy-start.3
  3.2 0.0 copy-done.2
  3.2 1.4 copy.48.tokens
  4.7 0.0 copy-done.3
  4.7 0.0 copy-start.9
  4.7 0.0 copy-start.10
  4.7 1.4 copy.49.cotangent
  6.1 0.0 copy-done.9
  6.1 0.6 reshape.103.positions
  6.7 0.0 copy-done.10
  6.7 0.7 jit_solution_.3.turns
  7.4 95.6 %shard_map.413 = (bf16[2,512,576]{2,1,0:T(8,128)(2,1)}, bf16[2,512,576]{2,1,0:T(8,128)(2,1)}, bf16[2,9,64,512]{3,2,1,0:T(8,128)(2,1)}, bf16[4,6,64,512]{3,2,1,0:...) custom-call(bf16[2,512,576]{2,1,0:T(8,128)(2,1)} %copy.48.tokens, ...), custom_call_target="tpu_custom_call" | custom-call | tf_op jit(solution)/shard_map/pallas_call | solution.py:613
  103.0 37.7 %shard_map.414 = (bf16[1024,576]{1,0:T(8,128)(2,1)}, f32[1024,576]{1,0:T(8,128)}, bf16[2,576,512]{2,1,0:T(8,128)(2,1)}, bf16[576,4096]{1,0:T(8,128)(2,1)}, bf16[1536,576]{1,0:T(8,128)(2,1)}) custom-call(bf16[1024,576]{1,0:T(8,128)(2,1)} %bitcast.22, bf16[2,576,512]{2,1,0:T(8,128)(2,1)} %bitcast.23, bf16[1024,576]{1,0:T(8,128)(2,1)} %bitcast.28, ...), custom_call_target="tpu_custom_call" | custom-call | tf_op jit(solution)/shard_map/pallas_call | solution.py:733
  140.7 0.0 copy-start.7
  140.7 123.5 %shard_map.415 = (bf16[2,512,576]{2,1,0:T(8,128)(2,1)}, bf16[2,512,576]{2,1,0:T(8,128)(2,1)}, bf16[144,4096]{1,0:T(8,128)(2,1)}, bf16[384,576]{1,0:T(8,128)(2,1)}, bf16[144,1024]{1,0:T(8,128)(2,1)}) custom-call(bf16[2,9,64,512]{3,2,1,0:T(8,128)(2,1)} %get-tuple-element.72.q_ref, bf16[4,6,64,512]{3,2,1,0:T(8,128)(2,1)} %get-tuple-element.73.kv, ...), custom_call_target="tpu_custom_call" | custom-call | tf_op jit(solution)/shard_map/pallas_call | solution.py:980
  264.3 0.0 copy-start.8
  264.3 0.0 copy-done.7
  264.3 1.3 copy.52.refs_11_
  265.6 0.0 copy-done.8
  265.6 1.3 copy.53.refs_17_
  266.8 12.7 %shard_map.416 = (f32[1,144]{1,0:T(1,128)}, f32[144,960]{1,0:T(8,128)}, f32[144,576]{1,0:T(8,128)}, f32[1,144]{1,0:T(1,128)}, f32[144,3072]{1,0:T(8,128)}, /*ind...) custom-call(bf16[144,4096]{1,0:T(8,128)(2,1)} %get-tuple-element.91., ...), custom_call_target="tpu_custom_call" | custom-call | tf_op jit(solution)/shard_map/pallas_call | solution.py:1045
  279.6 0.0 copy-start.6
  279.6 2.5 copy.56
  282.1 0.0 copy-start.5
  282.1 0.0 copy-done.6
  282.1 1.2 copy.57
  283.4 0.0 copy-start.4
  283.4 0.0 copy-done.5
  283.4 1.2 copy.58
  284.6 0.0 copy-start.1
  284.6 0.0 copy-done.4
  284.6 1.2 copy.59
  285.8 0.0 copy-start
  285.8 0.2 copy-done.1
  286.1 1.4 copy.54
  287.5 0.0 copy-done
  287.5 1.4 copy.55
Async XLA Ops:
  0.7 2.6 copy-start.2
  3.2 1.4 copy-start.3
  4.7 1.4 copy-start.9
  4.7 2.0 copy-start.10
  140.7 123.5 %copy-start.7 = (f32[384,576]{0,1:T(8,128)S(1)}, f32[384,576]{0,1:T(8,128)}, u32[]{:S(2)}) copy-start(f32[384,576]{0,1:T(8,128)} %param.36) | copy-start | bytes 2654212
  264.3 1.3 copy-start.8
  279.6 2.5 copy-start.6
  282.1 1.2 copy-start.5
  283.4 1.2 copy-start.4
  284.6 1.5 copy-start.1
  285.8 1.6 copy-start
